TPU v7x, 256 devices: a whole 4x4x8 slice. The times are simulated.
256 devices in a mesh: los: 32 (over x, z), sky: 8 (over y, core).
Axes of the slice: x: 4, y: 4, z: 8, core: 2. Of those that a mesh axis runs over, the one named last changes fastest.
Arguments:
- potentials: bfloat16 [128, 128, 4096], P('los', 'sky'), may hold values from -6 to 6
- shell_weight: float32 [128], P('los'), may hold values from 0.004 to 0.02
- shell_dist: float32 [128], P('los'), may hold values from 1 to 6.12, as said below
- source_dist: float32 [128], P('los'), may hold values from 1 to 6.12, as said below
Outputs:
- convergence: bfloat16 [128, 128, 4096], P('los', 'sky')
- shear_one: bfloat16 [128, 128, 4096], P('los', 'sky')
- shear_two: bfloat16 [128, 128, 4096], P('los', 'sky')
Inputs may be any that keep to these rules, and one draw needn't show every extreme that they name: shell_dist rises strictly with the shell index. source_dist[s] lies strictly between shell_dist[s] and shell_dist[s + 1].
All inputs are finite; a program needn't handle non-finite values.
Results may differ from a plain program's by a relative error of at most 0.001.
Values may be sent and summed in bfloat16 or wider, within the bound.
No kernel may reach another device: no remote copies, remote signals or barrier semaphores. Data moves between devices by JAX's collectives and lax.ppermute only.
A program may use at most 64 MiB of HBM per device.

v0:
```python
import jax
import jax.numpy as jnp
from jax import lax
from jax.sharding import PartitionSpec as P


def with_halo(cells, sides, width):
    for axis, dim in sides:
        count = lax.axis_size(axis)
        head = lax.slice_in_dim(cells, 0, width, axis=dim)
        tail = lax.slice_in_dim(cells, cells.shape[dim] - width, cells.shape[dim], axis=dim)
        cells = jnp.concatenate(
            [
                lax.ppermute(tail, axis, [(i, (i + 1) % count) for i in range(count)]),
                cells,
                lax.ppermute(head, axis, [((i + 1) % count, i) for i in range(count)]),
            ],
            axis=dim,
        )
    return cells


def first_cols(field):
    return (
        jnp.roll(field, 2, axis=-1)
        - 8.0 * jnp.roll(field, 1, axis=-1)
        + 8.0 * jnp.roll(field, -1, axis=-1)
        - jnp.roll(field, -2, axis=-1)
    ) / 12.0


def second_cols(field):
    return (
        -jnp.roll(field, 2, axis=-1)
        + 16.0 * jnp.roll(field, 1, axis=-1)
        - 30.0 * field
        + 16.0 * jnp.roll(field, -1, axis=-1)
        - jnp.roll(field, -2, axis=-1)
    ) / 12.0


def first_rows(padded, height):
    return (
        padded[:, 0:height, :]
        - 8.0 * padded[:, 1 : height + 1, :]
        + 8.0 * padded[:, 3 : height + 3, :]
        - padded[:, 4 : height + 4, :]
    ) / 12.0


def second_rows(padded, height):
    return (
        -padded[:, 0:height, :]
        + 16.0 * padded[:, 1 : height + 1, :]
        - 30.0 * padded[:, 2 : height + 2, :]
        + 16.0 * padded[:, 3 : height + 3, :]
        - padded[:, 4 : height + 4, :]
    ) / 12.0


def local_sums(potential, near_weight, far_weight):
    field = potential.astype(jnp.float32)
    local_near = jnp.cumsum(near_weight[:, None, None] * field, axis=0)
    local_far = jnp.cumsum(far_weight[:, None, None] * field, axis=0)
    return (local_near, local_far)


def nearer_sums(total_near, total_far):
    stacked = jnp.stack((total_near, total_far))[None]
    received = lax.all_to_all(stacked, "los", split_axis=3, concat_axis=0, tiled=True)
    earlier = jnp.cumsum(received, axis=0) - received
    result = lax.all_to_all(earlier, "los", split_axis=0, concat_axis=3, tiled=True)
    return (result[0, 0], result[0, 1])


def lens_from(local_near, local_far, prefix, source_dist):
    running_near = prefix[0][None] + local_near
    running_far = prefix[1][None] + local_far
    return running_near - running_far / source_dist[:, None, None]


def on_device(potentials, shell_weight, shell_dist, source_dist):
    height = potentials.shape[1]
    near_weight = shell_weight * shell_dist
    far_weight = near_weight * shell_dist
    local_near, local_far = local_sums(potentials, near_weight, far_weight)
    prefix = nearer_sums(local_near[-1], local_far[-1])
    lens_map = lens_from(local_near, local_far, prefix, source_dist)
    padded = with_halo(lens_map, (("sky", 1),), 2)
    interior = padded[:, 2 : height + 2, :]
    second_x = second_cols(interior)
    second_y = second_rows(padded, height)
    cross = first_rows(first_cols(padded), height)
    convergence = (0.5 * (second_x + second_y)).astype(jnp.bfloat16)
    shear_one = (0.5 * (second_x - second_y)).astype(jnp.bfloat16)
    shear_two = cross.astype(jnp.bfloat16)
    return (convergence, shear_one, shear_two)


def solution(mesh):
    return jax.shard_map(
        on_device,
        mesh=mesh,
        in_specs=(P("los", "sky", None), P("los"), P("los"), P("los")),
        out_specs=(P("los", "sky", None), P("los", "sky", None), P("los", "sky", None)),
        check_vma=False,
    )
```

profile of v0, /device:TPU:32, one launch (start us, length us, event | category | flops | bytes accessed | tf_op | source)
XLA Modules:
  0.0 103.1 jit_solution(17439832646547839495)
XLA Ops:
  0.6 0.7 fusion.27
  1.4 1.2 %fusion.2 = f32[4,16,4096]{2,1,0:T(8,128)S(1)} fusion(bf16[4,16,4096]{2,1,0:T(8,128)(2,1)} %param.4, f32[4]{0:T(128)S(1)} %get-tuple-element.15), kind=kOutput, calls=%fused_computation.15 | output fusion | flops 1310720 | bytes 1572880 | tf_op jit(solution)/shard_map/jit(cumsum)/reduce_window_sum | solution.py:64
  2.6 0.2 fusion.1
  2.9 4.4 %copy.83 = f32[1,2,16,4096]{2,1,0,3:T(2,128)} copy(f32[1,2,16,4096]{3,2,1,0:T(8,128)S(1)} %maximum_bitcast_fusion) | data formatting | bytes 1048576 | tf_op jit(solution)/shard_map/broadcast_in_dim | solution.py:69
  7.2 7.3 %reshape.11 = f32[32,1,4096]{2,1,0:T(1,128)S(1)} reshape(f32[4096,1,2,16]{3,2,1,0:T(2,128)} %bitcast.18) | data formatting | bytes 1048576
  14.6 28.6 %all_to_all.36 = f32[32,1,4096]{2,1,0:T(1,128)S(1)} all-to-all(f32[32,1,4096]{2,1,0:T(1,128)S(1)} %reshape.11), channel_id=1, replica_groups=mesh['los'=32,'sky'=8] {'los'}, dimensions={0} | all-to-all | bytes 1048576 | tf_op jit(solution)/shard_map/all_to_all | solution.py:70
  43.2 0.5 broadcast.48
  43.7 1.9 %reduce = f32[32,4096]{1,0:T(8,128)S(1)} reduce(f32[32,1,4096]{2,1,0:T(1,128)S(1)} %all_to_all.36, f32[]{:T(128)} %broadcast.48), dimensions={1}, to_apply=%all_to_all.26.reduce_sub_computation | reduce | bytes 1048580 | tf_op jit(solution)/shard_map/all_to_all | solution.py:70
  45.6 6.9 %reshape.12 = f32[4096,1,2,16]{3,2,1,0:T(2,128)} reshape(f32[32,4096]{1,0:T(8,128)S(1)} %reduce) | data formatting | bytes 1048576
  52.5 5.1 %copy.85 = f32[1,2,16,32,128]{4,2,1,3,0:T(8,128)S(1)} copy(f32[1,2,16,32,128]{2,1,4,3,0:T(2,128)} %bitcast.19) | data formatting | bytes 1048576 | tf_op jit(solution)/shard_map/all_to_all | solution.py:70
  57.6 4.1 %reduce-window_subtract_fusion = f32[32,2,16,128]{3,2,1,0:T(8,128)S(1)} fusion(f32[1,2,16,32,128]{4,2,1,3,0:T(8,128)S(1)} %copy.85), kind=kOutput, calls=%fused_computation.47 | output fusion | flops 4194304 | bytes 1048576 | tf_op jit(solution)/shard_map/jit(cumsum)/reduce_window_sum | solution.py:71
  61.7 21.6 %all_to_all.37 = f32[32,2,16,128]{3,2,1,0:T(8,128)S(1)} all-to-all(f32[32,2,16,128]{3,2,1,0:T(8,128)S(1)} %reduce-window_subtract_fusion), channel_id=1, replica_groups=mesh['los'=32,'sky'=8] {'los'}, dimensions={0} | all-to-all | bytes 1048576 | tf_op jit(solution)/shard_map/all_to_all | solution.py:72
  83.3 0.3 copy.86
  83.7 0.3 copy_bitcast_fusion
  84.0 0.3 copy-done.1
  84.3 0.3 divide_subtract_fusion
  84.8 0.4 fusion.33
  85.1 0.4 fusion.35
  85.7 0.5 collective-permute-start
  86.3 5.2 %collective-permute-done = f32[4,2,4096]{2,0,1:T(4,128)S(1)} collective-permute-done((f32[4,2,4096]{2,0,1:T(4,128)S(1)}, f32[4,2,4096]{2,0,1:T(4,128)S(1)}, u32[]{:S(2)}, u32[]{:S(2)}) %collective-permute-start) | collective-permute-done | bytes 131104 | tf_op jit(solution)/shard_map/ppermute | solution.py:14
  91.5 0.7 copy_dynamic-update-slice_fusion
  92.4 0.8 fusion.31
  93.2 0.8 fusion.28
  94.1 0.3 pad_maximum_fusion.1
  94.4 0.4 pad_maximum_fusion
  94.8 1.4 %maximum_subtract_fusion = f32[4,20,4096]{2,0,1:T(4,128)S(1)} fusion(f32[4,20,4094]{2,0,1:T(4,128)S(1)} %get-tuple-element.23, f32[4,20,2]{2,0,1:T(4,128)S(1)} %get-tuple-element.21, f32[4,20,4095]{2,0,1:T(4,128)S(1)} %get-tuple-element.18, f32[4,20,1]{2,0,1:T(4,128)S(1)} %get-tuple-element.20), kind=kLoop, calls=%fused_computation.10 | loop fusion | flops 1310720 | bytes 3932160 | tf_op jit(solution)/shard_map/sub | solution.py:25
  96.2 2.3 %fusion = f32[4,20,4096]{2,1,0:T(8,128)S(1)} fusion(f32[4,20,4096]{2,0,1:T(4,128)S(1)} %pad_maximum_fusion.1, f32[4,20,4096]{2,0,1:T(4,128)S(1)} %maximum_subtract_fusion, f32[4,20,4096]{2,0,1:T(4,128)S(1)} %pad_maximum_fusion), kind=kLoop, calls=%fused_computation.5 | loop fusion | flops 1310720 | bytes 5242880 | tf_op jit(solution)/shard_map/div | solution.py:24
  98.5 1.2 %fusion.13 = bf16[4,16,4096]{2,1,0:T(8,128)(2,1)} fusion(f32[4,20,4096]{2,1,0:T(8,128)S(1)} %fusion), kind=kLoop, calls=%fused_computation.27 | loop fusion | flops 1835008 | bytes 4718592 | tf_op jit(solution)/shard_map/convert_element_type | solution.py:96
  99.8 0.1 copy.90
  99.9 0.1 copy.88
  100.0 2.2 %multiply_convert_fusion = (bf16[4,16,4096]{2,1,0:T(8,128)(2,1)}, f32[4,16,4096]{2,1,0:T(8,128)S(1)}, f32[4,16,4096]{2,1,0:T(8,128)S(1)}) fusion(f32[4,2,4096]{2,1,0:T(2,128)S(1)} %copy.90, f32[4,16,4096]{2,1,0:T(8,128)S(1)} %divide_subtract_fusion, f32[4,2,4096]{2,1,0:T(2,128)S(1)} %copy.88, f32[4,16,2]{2,1,0:T(8,128)S(1)} %get-tuple-element.26, ...), kind=kLoop, calls=%fused_computation.44 | loop fusion | flops 7340032 | bytes 8126464 | tf_op jit(solution)/shard_map/convert_element_type | solution.py:95
  102.2 0.9 multiply_convert_fusion.1
  (18 shorter events, 0.8 us)
Async XLA Ops:
  0.6 2.0 %copy-start = (bf16[4,16,4096]{2,1,0:T(8,128)(2,1)S(1)}, bf16[4,16,4096]{2,1,0:T(8,128)(2,1)}, u32[]{:S(2)}) copy-start(bf16[4,16,4096]{2,1,0:T(8,128)(2,1)} %param.4) | copy-start | bytes 1572868
  83.6 0.7 copy-start.1
  85.6 6.7 %collective-permute-start.1 = (f32[4,2,4096]{2,0,1:T(4,128)S(1)}, f32[4,2,4096]{2,0,1:T(4,128)S(1)}, u32[]{:S(2)}, u32[]{:S(2)}) collective-permute-start(f32[4,2,4096]{2,0,1:T(4,128)S(1)} %copy.89), channel_id=1, source_target_pairs={{1,0},{2,1},{3,2},{4,3},{5,4},{6,5},{7,6},{0,7},{9,8},{10,9},{11,1... | collective-permute-start | bytes 393224 | tf_op jit(solution)/shard_map/ppermute | solution.py:16
  85.7 5.8 %collective-permute-start = (f32[4,2,4096]{2,0,1:T(4,128)S(1)}, f32[4,2,4096]{2,0,1:T(4,128)S(1)}, u32[]{:S(2)}, u32[]{:S(2)}) collective-permute-start(f32[4,2,4096]{2,0,1:T(4,128)S(1)} %copy.87), channel_id=1, source_target_pairs={{0,1},{1,2},{2,3},{3,4},{4,5},{5,6},{6,7},{7,0},{8,9},{9,10},{10,1... | collective-permute-start | bytes 393224 | tf_op jit(solution)/shard_map/ppermute | solution.py:14
where the time goes:
time: 103 us
  blocking collectives  50.2 us (49%)
  local copies, waits for them, and re-layouts  29.1 us (28%)
  other arithmetic  17.2 us (17%)
  waiting for transfers between devices  5.2 us (5%)
    all_to_all x1, blocking collectives, nearer_sums(): lax.all_to_all(stacked, 'los', split_axis=3, concat_axis=0, tiled=True)  28.6 us
    all_to_all x1, blocking collectives, nearer_sums(): lax.all_to_all(earlier, 'los', split_axis=0, concat_axis=3, tiled=True)  21.6 us
    unnamed x9, local copies, waits for them, and re-layouts  15.6 us
    all_to_all x2, local copies, waits for them, and re-layouts, nearer_sums(): lax.all_to_all(stacked, 'los', split_axis=3, concat_axis=0, tiled=True)  5.62 us
    ppermute x1, waiting for transfers between devices, with_halo(): lax.ppermute(tail, axis, [(i, (i + 1) % count) for i in range(count)])  5.2 us
    broadcast_in_dim x1, local copies, waits for them, and re-layouts, nearer_sums(): stacked = jnp.stack((total_near, total_far))[None]  4.39 us
    another operation x1, other arithmetic, nearer_sums(): earlier = jnp.cumsum(received, axis=0) - received  4.06 us
    div x1, other arithmetic, first_cols(): (jnp.roll(field, 2, axis=-1) - 8.0 * jnp.roll(field, 1, axis=-1) + 8.0 *...  2.3 us
  transfers between devices with their start and end apart: 2, of which 1 were waited for; matrix products, arithmetic and copies ran while one was open for 1% of the time, Pallas kernels for 0%

commit v1 on v0

v1 whole, which is shorter than its diff:
```python
import functools

import jax
import jax.numpy as jnp
from jax import lax
from jax.experimental import pallas as pl
from jax.experimental.pallas import tpu as pltpu
from jax.sharding import PartitionSpec as P

LANES = 128
SUB = 8
VMEM = pl.BlockSpec(memory_space=pltpu.VMEM)
SMEM = pl.BlockSpec(memory_space=pltpu.SMEM)


def params():
    return pltpu.CompilerParams(vmem_limit_bytes=40 * 1024 * 1024)


def cost(flops, nbytes):
    return pl.CostEstimate(flops=flops, bytes_accessed=nbytes, transcendentals=0)


def totals_kernel(near_ref, far_ref, pot_ref, out_ref):
    shells = pot_ref.shape[0]
    chunks = out_ref.shape[0]
    near = [near_ref[j] for j in range(shells)]
    far = [far_ref[j] for j in range(shells)]

    def one(c, carry):
        cols = pl.ds(pl.multiple_of(c * LANES, LANES), LANES)
        total_near = total_far = None
        for j in range(shells):
            field = pot_ref[j, :, cols].astype(jnp.float32)
            total_near = near[j] * field if j == 0 else total_near + near[j] * field
            total_far = far[j] * field if j == 0 else total_far + far[j] * field
        out_ref[c, 0] = total_near
        out_ref[c, 1] = total_far
        return carry

    lax.fori_loop(0, chunks, one, 0, unroll=4)


def earlier_kernel(in_ref, out_ref):
    count, per = in_ref.shape[0], in_ref.shape[1]
    for q in range(per):
        for f in range(2):
            run = jnp.zeros(in_ref.shape[3:], jnp.float32)
            for i in range(count):
                out_ref[i, q, f] = run
                if i < count - 1:
                    run = run + in_ref[i, q, f]


def own_kernel(near_ref, far_ref, inv_ref, pot_ref, pre_ref, plus_ref, minus_ref, cross_ref, lens):
    planes = pot_ref.shape[0]
    chunks = pre_ref.shape[0]
    near = [near_ref[j] for j in range(planes)]
    far = [far_ref[j] for j in range(planes)]
    inv = [inv_ref[j] for j in range(planes)]
    rows = pot_ref.shape[1]

    def build(c, carry):
        cols = pl.ds(pl.multiple_of(c * LANES, LANES), LANES)
        run_near = pre_ref[c, 0]
        run_far = pre_ref[c, 1]
        for s in range(planes):
            field = pot_ref[s, :, cols].astype(jnp.float32)
            run_near = run_near + near[s] * field
            run_far = run_far + far[s] * field
            lens[s, c] = run_near - run_far * inv[s]
        return carry

    lax.fori_loop(0, chunks, build, 0, unroll=2)
    lane = lax.broadcasted_iota(jnp.int32, (rows, LANES), 1)
    row = lax.broadcasted_iota(jnp.int32, (rows, LANES), 0)

    def sten(c, carry):
        before = lax.rem(c + chunks - 1, chunks)
        after = lax.rem(c + 1, chunks)
        for s in range(planes):
            here = lens[s, c]
            prev = lens[s, before]
            nxt = lens[s, after]
            r1 = pltpu.roll(jnp.where(lane == LANES - 1, prev, here), 1, 1)
            r2 = pltpu.roll(jnp.where(lane >= LANES - 2, prev, here), 2, 1)
            l1 = pltpu.roll(jnp.where(lane == 0, nxt, here), LANES - 1, 1)
            l2 = pltpu.roll(jnp.where(lane < 2, nxt, here), LANES - 2, 1)
            first = 8.0 * (l1 - r1) - (l2 - r2)
            sx = 16.0 * (l1 + r1) - (l2 + r2)

            def down(f, k):
                return jnp.where(row < k, 0.0, pltpu.roll(f, k, 0))

            def up(f, k):
                return jnp.where(row >= rows - k, 0.0, pltpu.roll(f, rows - k, 0))

            sy = 16.0 * (up(here, 1) + down(here, 1)) - (up(here, 2) + down(here, 2))
            plus_ref[s, c] = (sx + sy) - 60.0 * here
            minus_ref[s, c] = sx - sy
            cross_ref[s, c] = 8.0 * (up(first, 1) - down(first, 1)) - (up(first, 2) - down(first, 2))
        return carry

    lax.fori_loop(0, chunks, sten, 0)


def edge_kernel(near_ref, far_ref, inv_ref, pot_ref, pre_ref, plus_ref, minus_ref, cross_ref,
                conv_ref, one_ref, two_ref, lens):
    planes = pot_ref.shape[0]
    chunks = pre_ref.shape[0]
    near = [near_ref[j] for j in range(planes)]
    far = [far_ref[j] for j in range(planes)]
    inv = [inv_ref[j] for j in range(planes)]
    rows = plus_ref.shape[2]

    def build(c, carry):
        cols = pl.ds(pl.multiple_of(c * LANES, LANES), LANES)
        run_near = pre_ref[c, 0]
        run_far = pre_ref[c, 1]
        for s in range(planes):
            field = pot_ref[s, :, cols].astype(jnp.float32)
            run_near = run_near + near[s] * field
            run_far = run_far + far[s] * field
            lens[s, c] = run_near - run_far * inv[s]
        return carry

    lax.fori_loop(0, chunks, build, 0, unroll=2)
    lane = lax.broadcasted_iota(jnp.int32, (SUB, LANES), 1)
    row = lax.broadcasted_iota(jnp.int32, (SUB, LANES), 0)

    def sten(c, carry):
        before = lax.rem(c + chunks - 1, chunks)
        after = lax.rem(c + 1, chunks)
        cols = pl.ds(pl.multiple_of(c * LANES, LANES), LANES)
        for s in range(planes):
            here = lens[s, c]
            prev = lens[s, before]
            nxt = lens[s, after]
            r1 = pltpu.roll(jnp.where(lane == LANES - 1, prev, here), 1, 1)
            r2 = pltpu.roll(jnp.where(lane >= LANES - 2, prev, here), 2, 1)
            l1 = pltpu.roll(jnp.where(lane == 0, nxt, here), LANES - 1, 1)
            l2 = pltpu.roll(jnp.where(lane < 2, nxt, here), LANES - 2, 1)
            first = 8.0 * (l1 - r1) - (l2 - r2)

            def top(f):
                d1 = jnp.where(row < 1, pltpu.roll(f, 1, 0), 0.0)
                d2 = jnp.where(row < 2, pltpu.roll(f, 2, 0), 0.0)
                return d1, d2

            def bottom(f):
                u1 = jnp.where(row >= SUB - 1, pltpu.roll(f, SUB - 1, 0), 0.0)
                u2 = jnp.where(row >= SUB - 2, pltpu.roll(f, SUB - 2, 0), 0.0)
                return u1, u2

            d1, d2 = top(here)
            u1, u2 = bottom(here)
            middle = [jnp.zeros((rows - 2 * SUB, LANES), jnp.float32)] if rows > 2 * SUB else []
            sy = jnp.concatenate([16.0 * d1 - d2, *middle, 16.0 * u1 - u2], 0)
            d1, d2 = top(first)
            u1, u2 = bottom(first)
            cross = jnp.concatenate([d2 - 8.0 * d1, *middle, 8.0 * u1 - u2], 0)
            conv_ref[s, :, cols] = ((plus_ref[s, c] + sy) * (1.0 / 24.0)).astype(jnp.bfloat16)
            one_ref[s, :, cols] = ((minus_ref[s, c] - sy) * (1.0 / 24.0)).astype(jnp.bfloat16)
            two_ref[s, :, cols] = ((cross_ref[s, c] + cross) * (1.0 / 144.0)).astype(jnp.bfloat16)
        return carry

    lax.fori_loop(0, chunks, sten, 0)


def on_device(potentials, shell_weight, shell_dist, source_dist):
    shells, height, width = potentials.shape
    chunks = width // LANES
    count = lax.axis_size("los")
    sky = lax.axis_size("sky")
    forward = [(i, (i + 1) % sky) for i in range(sky)]
    backward = [((i + 1) % sky, i) for i in range(sky)]
    near = shell_weight * shell_dist
    far = near * shell_dist
    inv = 1.0 / source_dist
    piece = (2, height, LANES)
    f32 = functools.partial(jax.ShapeDtypeStruct, dtype=jnp.float32)

    pot_before = lax.ppermute(potentials[:, height - 2 :], "sky", forward)
    pot_after = lax.ppermute(potentials[:, :2], "sky", backward)

    totals = pl.pallas_call(
        totals_kernel,
        out_shape=f32((chunks,) + piece),
        in_specs=[SMEM, SMEM, VMEM],
        out_specs=VMEM,
        compiler_params=params(),
        cost_estimate=cost(4 * potentials.size, 6 * potentials.size),
    )(near, far, potentials)
    received = lax.all_to_all(totals, "los", split_axis=0, concat_axis=0, tiled=True)
    earlier = pl.pallas_call(
        earlier_kernel,
        out_shape=f32((count, chunks // count) + piece),
        in_specs=[VMEM],
        out_specs=VMEM,
        compiler_params=params(),
        cost_estimate=cost(totals.size, 8 * totals.size),
    )(received.reshape((count, chunks // count) + piece))
    prefix = lax.all_to_all(earlier.reshape((chunks,) + piece), "los", split_axis=0, concat_axis=0, tiled=True)

    pre_before = lax.ppermute(prefix[:, :, height - 2 :], "sky", forward)
    pre_after = lax.ppermute(prefix[:, :, :2], "sky", backward)

    grids = [f32((shells, chunks, height, LANES))] * 3
    plus, minus, cross = pl.pallas_call(
        own_kernel,
        out_shape=grids,
        in_specs=[SMEM, SMEM, SMEM, VMEM, VMEM],
        out_specs=[VMEM] * 3,
        scratch_shapes=[pltpu.VMEM((shells, chunks, height, LANES), jnp.float32)],
        compiler_params=params(),
        cost_estimate=cost(60 * potentials.size, 20 * potentials.size),
    )(near, far, inv, potentials, prefix)

    pot_edge = jnp.concatenate([pot_after, jnp.zeros((shells, SUB - 4, width), potentials.dtype), pot_before], 1)
    pre_edge = jnp.concatenate([pre_after, jnp.zeros((chunks, 2, SUB - 4, LANES), jnp.float32), pre_before], 2)
    outs = [jax.ShapeDtypeStruct(potentials.shape, jnp.bfloat16)] * 3
    return tuple(
        pl.pallas_call(
            edge_kernel,
            out_shape=outs,
            in_specs=[SMEM, SMEM, SMEM, VMEM, VMEM, VMEM, VMEM, VMEM],
            out_specs=[VMEM] * 3,
            scratch_shapes=[pltpu.VMEM((shells, chunks, SUB, LANES), jnp.float32)],
            compiler_params=params(),
            cost_estimate=cost(40 * potentials.size, 20 * potentials.size),
        )(near, far, inv, pot_edge, pre_edge, plus, minus, cross)
    )


def solution(mesh):
    return jax.shard_map(
        on_device,
        mesh=mesh,
        in_specs=(P("los", "sky", None), P("los"), P("los"), P("los")),
        out_specs=(P("los", "sky", None), P("los", "sky", None), P("los", "sky", None)),
        check_vma=False,
    )
```

time: 103 us -> 67.3 us (0.65)
  the two profiles are of different devices: /device:TPU:32 before, /device:TPU:1 now
where the time goes in v1:
time: 67.3 us; the launch traced here: 67 us
  blocking collectives  26 us (39%)
  starting transfers between devices  16.2 us (24%)
  Pallas kernels  11.3 us (17%)
  waiting for transfers between devices  9.91 us (15%)
  local copies, waits for them, and re-layouts  1.94 us (3%)
  other arithmetic  0.93 us (1%)
  between operations  0.71 us (1%)
    all_to_all x1, blocking collectives, on_device(): lax.all_to_all(totals, 'los', split_axis=0, concat_axis=0, tiled=True)  26 us
    all_to_all x1, waiting for transfers between devices, on_device(): lax.all_to_all(earlier.reshape((chunks,) + piece), 'los', split_axis=0, c...  9.9 us
    all_to_all x1, starting transfers between devices, on_device(): lax.all_to_all(earlier.reshape((chunks,) + piece), 'los', split_axis=0, c...  7.62 us
    pallas_call x1, Pallas kernels, on_device(): pl.pallas_call(edge_kernel, out_shape=outs, in_specs=[SMEM, SMEM, SMEM, V...  5.04 us
    pallas_call x1, Pallas kernels, on_device(): pl.pallas_call(own_kernel, out_shape=grids, in_specs=[SMEM, SMEM, SMEM, V...  4.68 us
    ppermute x1, starting transfers between devices, on_device(): pre_after = lax.ppermute(prefix[:, :, :2], 'sky', backward)  4.56 us
    ppermute x1, starting transfers between devices, on_device(): pot_after = lax.ppermute(potentials[:, :2], 'sky', backward)  1.65 us
    unnamed x6, local copies, waits for them, and re-layouts  1.62 us
  transfers between devices with their start and end apart: 5, of which 1 were waited for; matrix products, arithmetic and copies ran while one was open for 1% of the time, Pallas kernels for 7%

profile of v1, /device:TPU:1, one launch (start us, length us, event | category | flops | bytes accessed | tf_op | source)
XLA Modules:
  0.0 67.0 jit_solution(10070354200365749038)
XLA Ops:
  0.6 0.7 %fusion = (f32[4]{0:T(128)S(1)}, f32[4]{0:T(128)S(1)}) fusion(f32[4]{0:T(128)} %param.6, f32[4]{0:T(128)} %param.5), kind=kLoop, calls=%fused_computation.3 | loop fusion | flops 8 | bytes 64 | tf_op jit(solution)/shard_map/mul | solution.py:178
  1.3 0.0 copy-start
  1.3 1.0 %copy-done = bf16[4,16,4096]{2,1,0:T(8,128)(2,1)S(1)} copy-done((bf16[4,16,4096]{2,1,0:T(8,128)(2,1)S(1)}, bf16[4,16,4096]{2,1,0:T(8,128)(2,1)}, u32[]{:S(2)}) %copy-start) | copy-done | bytes 524312
  2.3 0.8 %shard_map.67 = f32[32,2,16,128]{3,2,1,0:T(8,128)S(1)} custom-call(f32[4]{0:T(128)S(1)} %get-tuple-element.10.near_ref, f32[4]{0:T(128)S(1)} %get-tuple-element.9.far_ref, bf16[4,16,4096]{2,1,0:T(8,128)(2,1)S(1)} %copy-done), custom_call_target="tpu_custom_call" | custom-call | flops 1048576 | bytes 1572864 | tf_op jit(solution)/shard_map/pallas_call | solution.py:186
  3.1 26.0 %all_to_all.10 = f32[32,2,16,128]{3,2,1,0:T(8,128)S(1)} all-to-all(f32[32,2,16,128]{3,2,1,0:T(8,128)S(1)} %shard_map.67), channel_id=1, replica_groups=mesh['los'=32,'sky'=8] {'los'}, dimensions={0} | all-to-all | bytes 1048576 | tf_op jit(solution)/shard_map/all_to_all | solution.py:194
  29.1 0.8 %shard_map.68 = f32[32,1,2,16,128]{4,3,2,1,0:T(8,128)} custom-call(f32[32,1,2,16,128]{4,3,2,1,0:T(8,128)S(1)} %bitcast.2), custom_call_target="tpu_custom_call" | custom-call | flops 131072 | bytes 1048576 | tf_op jit(solution)/shard_map/pallas_call | solution.py:195
  29.9 0.0 copy-start.1
  29.9 7.6 %all-to-all-start.1 = ((f32[32,2,16,128]{3,2,1,0:T(8,128)}), f32[32,2,16,128]{3,2,1,0:T(8,128)S(1)}, u32[]{:S(2)}, u32[]{:S(2)}) async-start(f32[32,2,16,128]{3,2,1,0:T(8,128)} %bitcast.1), calls=%async_computation.1 | async-start | bytes 1048576 | tf_op jit(solution)/shard_map/all_to_all | solution.py:203
  37.6 0.0 copy-done.1
  37.6 0.1 fusion.2
  37.7 1.6 %collective-permute-start = (bf16[4,2,4096]{2,1,0:T(2,128)(2,1)S(1)}, bf16[4,2,4096]{2,1,0:T(2,128)(2,1)S(1)}, u32[]{:S(2)}, u32[]{:S(2)}) collective-permute-start(bf16[4,2,4096]{2,1,0:T(2,128)(2,1)S(1)} %get-tuple-element.13), channel_id=1, source_target_pairs={{1,0},{2,1},{3,2},{4,3},{5,4},{6,5},{7,6},{0,7},{9,8},{10,9},{11,1... | collective-permute-start | bytes 196616 | tf_op jit(solution)/shard_map/ppermute | solution.py:184
  39.3 1.2 %collective-permute-start.1 = (bf16[4,2,4096]{2,1,0:T(2,128)(2,1)S(1)}, bf16[4,2,4096]{2,1,0:T(2,128)(2,1)S(1)}, u32[]{:S(2)}, u32[]{:S(2)}) collective-permute-start(bf16[4,2,4096]{2,1,0:T(2,128)(2,1)S(1)} %get-tuple-element.14), channel_id=1, source_target_pairs={{0,1},{1,2},{2,3},{3,4},{4,5},{5,6},{6,7},{7,0},{8,9},{9,10},{10,1... | collective-permute-start | bytes 196616 | tf_op jit(solution)/shard_map/ppermute | solution.py:183
  40.5 0.1 pad.4.clone
  40.6 0.0 copy-start.2
  40.6 0.1 pad.1.clone
  40.7 0.6 copy-done.2
  41.3 9.9 %all-to-all-done.1.pre_ref = f32[32,2,16,128]{3,2,1,0:T(8,128)S(1)} async-done(((f32[32,2,16,128]{3,2,1,0:T(8,128)}), f32[32,2,16,128]{3,2,1,0:T(8,128)S(1)}, u32[]{:S(2)}, u32[]{:S(2)}) %all-to-all-start.1) | async-done | bytes 524320 | tf_op jit(solution)/shard_map/all_to_all | solution.py:203
  51.2 4.6 %collective-permute-start.2 = (f32[32,2,2,128]{3,2,1,0:T(2,128)S(1)}, f32[32,2,2,128]{3,2,1,0:T(2,128)S(1)}, u32[]{:S(2)}, u32[]{:S(2)}) collective-permute-start(f32[32,2,2,128]{3,2,1,0:T(2,128)S(1)} %get-tuple-element.11), channel_id=1, source_target_pairs={{1,0},{2,1},{3,2},{4,3},{5,4},{6,5},{7,6},{0,7},{9,8},{10,9},{11,1... | collective-permute-start | bytes 196616 | tf_op jit(solution)/shard_map/ppermute | solution.py:206
  55.8 1.2 %collective-permute-start.3 = (f32[32,2,2,128]{3,2,1,0:T(2,128)S(1)}, f32[32,2,2,128]{3,2,1,0:T(2,128)S(1)}, u32[]{:S(2)}, u32[]{:S(2)}) collective-permute-start(f32[32,2,2,128]{3,2,1,0:T(2,128)S(1)} %get-tuple-element.12), channel_id=1, source_target_pairs={{0,1},{1,2},{2,3},{3,4},{4,5},{5,6},{6,7},{7,0},{8,9},{9,10},{10,1... | collective-permute-start | bytes 196616 | tf_op jit(solution)/shard_map/ppermute | solution.py:205
  57.0 0.0 collective-permute-done
  57.0 0.0 collective-permute-done.1
  57.0 0.2 pad_maximum_fusion.pot_ref
  57.2 4.7 %shard_map.69 = (f32[4,32,16,128]{3,2,1,0:T(8,128)S(1)}, f32[4,32,16,128]{3,2,1,0:T(8,128)S(1)}, f32[4,32,16,128]{3,2,1,0:T(8,128)S(1)}) custom-call(f32[4]{0:T(128)S(1)} %get-tuple-element.10.near_ref, f32[4]{0:T(128)S(1)} %get-tuple-element.9.far_ref, f32[4]{0:T(128)S(1)} %broadcast_divide_fusion.inv_ref, bf16[4,16,4096]{2,1,0:T(8,128)(2,1)S(1)} %copy-done.1, ...), custom_call_target="tpu_custom_call" | custom-call | flops 15728640 | bytes 5242880 | tf_op jit(solution)/shard_map/pallas_call | solution.py:209
  61.9 0.0 collective-permute-done.2
  61.9 0.0 collective-permute-done.3
  61.9 0.1 pad_maximum_fusion.1.pre_ref
  62.0 5.0 %shard_map.70 = (bf16[4,16,4096]{2,1,0:T(8,128)(2,1)}, bf16[4,16,4096]{2,1,0:T(8,128)(2,1)}, bf16[4,16,4096]{2,1,0:T(8,128)(2,1)}) custom-call(f32[4]{0:T(128)S(1)} %get-tuple-element.10.near_ref, f32[4]{0:T(128)S(1)} %get-tuple-element.9.far_ref, f32[4]{0:T(128)S(1)} %broadcast_divide_fusion.inv_ref, bf16[4,8,4096]{2,1,0:T(8,128)(2,1)S(1)} %pad_maximum_fusion.pot_ref, ...), custom_call_target="tpu_custom_call" | custom-call | flops 10485760 | bytes 5242880 | tf_op jit(solution)/shard_map/pallas_call | solution.py:223
  (4 shorter events, 0.1 us)
Async XLA Ops:
  1.3 1.0 %copy-start = (bf16[4,16,4096]{2,1,0:T(8,128)(2,1)S(1)}, bf16[4,16,4096]{2,1,0:T(8,128)(2,1)}, u32[]{:S(2)}) copy-start(bf16[4,16,4096]{2,1,0:T(8,128)(2,1)} %pot_ref.3) | copy-start | bytes 1572868
  29.9 7.6 %copy-start.1 = (bf16[4,16,4096]{2,1,0:T(8,128)(2,1)S(1)}, bf16[4,16,4096]{2,1,0:T(8,128)(2,1)}, u32[]{:S(2)}) copy-start(bf16[4,16,4096]{2,1,0:T(8,128)(2,1)} %pot_ref.3) | copy-start | bytes 1572868
  29.9 21.2 %all-to-all-start.1 = ((f32[32,2,16,128]{3,2,1,0:T(8,128)}), f32[32,2,16,128]{3,2,1,0:T(8,128)S(1)}, u32[]{:S(2)}, u32[]{:S(2)}) async-start(f32[32,2,16,128]{3,2,1,0:T(8,128)} %bitcast.1), calls=%async_computation.1 | async-start | bytes 1048576 | tf_op jit(solution)/shard_map/all_to_all | solution.py:203
  37.7 19.3 %collective-permute-start = (bf16[4,2,4096]{2,1,0:T(2,128)(2,1)S(1)}, bf16[4,2,4096]{2,1,0:T(2,128)(2,1)S(1)}, u32[]{:S(2)}, u32[]{:S(2)}) collective-permute-start(bf16[4,2,4096]{2,1,0:T(2,128)(2,1)S(1)} %get-tuple-element.13), channel_id=1, source_target_pairs={{1,0},{2,1},{3,2},{4,3},{5,4},{6,5},{7,6},{0,7},{9,8},{10,9},{11,1... | collective-permute-start | bytes 196616 | tf_op jit(solution)/shard_map/ppermute | solution.py:184
  39.3 17.7 %collective-permute-start.1 = (bf16[4,2,4096]{2,1,0:T(2,128)(2,1)S(1)}, bf16[4,2,4096]{2,1,0:T(2,128)(2,1)S(1)}, u32[]{:S(2)}, u32[]{:S(2)}) collective-permute-start(bf16[4,2,4096]{2,1,0:T(2,128)(2,1)S(1)} %get-tuple-element.14), channel_id=1, source_target_pairs={{0,1},{1,2},{2,3},{3,4},{4,5},{5,6},{6,7},{7,0},{8,9},{9,10},{10,1... | collective-permute-start | bytes 196616 | tf_op jit(solution)/shard_map/ppermute | solution.py:183
  40.6 0.7 copy-start.2
  51.2 10.6 %collective-permute-start.2 = (f32[32,2,2,128]{3,2,1,0:T(2,128)S(1)}, f32[32,2,2,128]{3,2,1,0:T(2,128)S(1)}, u32[]{:S(2)}, u32[]{:S(2)}) collective-permute-start(f32[32,2,2,128]{3,2,1,0:T(2,128)S(1)} %get-tuple-element.11), channel_id=1, source_target_pairs={{1,0},{2,1},{3,2},{4,3},{5,4},{6,5},{7,6},{0,7},{9,8},{10,9},{11,1... | collective-permute-start | bytes 196616 | tf_op jit(solution)/shard_map/ppermute | solution.py:206
  55.8 6.1 %collective-permute-start.3 = (f32[32,2,2,128]{3,2,1,0:T(2,128)S(1)}, f32[32,2,2,128]{3,2,1,0:T(2,128)S(1)}, u32[]{:S(2)}, u32[]{:S(2)}) collective-permute-start(f32[32,2,2,128]{3,2,1,0:T(2,128)S(1)} %get-tuple-element.12), channel_id=1, source_target_pairs={{0,1},{1,2},{2,3},{3,4},{4,5},{5,6},{6,7},{7,0},{8,9},{9,10},{10,1... | collective-permute-start | bytes 196616 | tf_op jit(solution)/shard_map/ppermute | solution.py:205

commit v2 on v1

v2 whole, which is shorter than its diff:
```python
import functools

import jax
import jax.numpy as jnp
from jax import lax
from jax.experimental import pallas as pl
from jax.experimental.pallas import tpu as pltpu
from jax.sharding import PartitionSpec as P

LANES = 128
SUB = 8
STEPS = 4
VMEM = pl.BlockSpec(memory_space=pltpu.VMEM)
SMEM = pl.BlockSpec(memory_space=pltpu.SMEM)
F32 = jnp.float32
BF16 = jnp.bfloat16


def params(mib=24):
    return pltpu.CompilerParams(vmem_limit_bytes=mib * 1024 * 1024)


def cost(flops, nbytes):
    return pl.CostEstimate(flops=flops, bytes_accessed=nbytes, transcendentals=0)


def f32(*shape):
    return jax.ShapeDtypeStruct(shape, F32)


def columns(c):
    return pl.ds(pl.multiple_of(c * LANES, LANES), LANES)


def split(value):
    high = value.astype(BF16)
    return high, (value - high.astype(F32)).astype(BF16)


def iotas():
    shape = (SUB, LANES)
    return lax.broadcasted_iota(jnp.int32, shape, 0), lax.broadcasted_iota(jnp.int32, shape, 1)


def along_x(prev, here, nxt, lane):
    r1 = pltpu.roll(jnp.where(lane == LANES - 1, prev, here), 1, 1)
    r2 = pltpu.roll(jnp.where(lane >= LANES - 2, prev, here), 2, 1)
    l1 = pltpu.roll(jnp.where(lane == 0, nxt, here), LANES - 1, 1)
    l2 = pltpu.roll(jnp.where(lane < 2, nxt, here), LANES - 2, 1)
    return 8.0 * (l1 - r1) - (l2 - r2), 16.0 * (l1 + r1) - (l2 + r2)


def shifts_y(tiles, edge, row):
    count = len(tiles)
    out = []
    for k in range(count):
        above = edge if k == 0 else tiles[k - 1]
        below = edge if k == count - 1 else tiles[k + 1]
        here = tiles[k]
        d1 = pltpu.roll(jnp.where(row == SUB - 1, above, here), 1, 0)
        d2 = pltpu.roll(jnp.where(row >= SUB - 2, above, here), 2, 0)
        u1 = pltpu.roll(jnp.where(row == 0, below, here), SUB - 1, 0)
        u2 = pltpu.roll(jnp.where(row < 2, below, here), SUB - 2, 0)
        out.append((d1, d2, u1, u2))
    return out


def second_y(d1, d2, u1, u2):
    return 16.0 * (u1 + d1) - (u2 + d2)


def first_y(d1, d2, u1, u2):
    return 8.0 * (u1 - d1) - (u2 - d2)


def spread(ref, shape):
    return [jnp.full(shape, ref[j], F32) for j in range(ref.shape[0])]


def weights(weight_ref, dist_ref, shape):
    dist = spread(dist_ref, shape)
    near = [w * d for w, d in zip(spread(weight_ref, shape), dist)]
    return dist, near


def inverses(source_ref, shape):
    inv = [1.0 / d for d in spread(source_ref, shape)]
    return inv, rounded(0.5 * (inv[0] + inv[-1]))


def rounded(value):
    return value.astype(BF16).astype(F32)


def totals_kernel(weight_ref, dist_ref, source_ref, pot_ref, out_ref):
    shells, height = pot_ref.shape[0], pot_ref.shape[1]
    shape = (height, LANES)
    dist, near = weights(weight_ref, dist_ref, shape)
    dist_mid = rounded(0.5 * (dist[0] + dist[-1]))
    off = [n * (d - dist_mid) for n, d in zip(near, dist)]
    _, inv_mid = inverses(source_ref, shape)
    row = lax.broadcasted_iota(jnp.int32, shape, 0)
    lane = lax.broadcasted_iota(jnp.int32, shape, 1)
    first = (row == 0) & (lane == 0)
    second = (row == 0) & (lane == 1)

    def one(c, carry):
        total_near = total_off = None
        for j in range(shells):
            field = pot_ref[j, :, columns(c)].astype(F32)
            total_near = near[j] * field if j == 0 else total_near + near[j] * field
            total_off = off[j] * field if j == 0 else total_off + off[j] * field
        high = total_near.astype(BF16)
        low = total_near - high.astype(F32)
        out_ref[c, 0] = high
        out_ref[c, 1] = jnp.where(first, dist_mid, jnp.where(second, inv_mid, low)).astype(BF16)
        out_ref[c, 2] = total_off.astype(BF16)
        return carry

    lax.fori_loop(0, out_ref.shape[0], one, 0, unroll=4)


def earlier_kernel(in_ref, out_ref):
    count, per = in_ref.shape[0], in_ref.shape[1]
    shape = in_ref.shape[3:]
    row = lax.broadcasted_iota(jnp.int32, shape, 0)
    lane = lax.broadcasted_iota(jnp.int32, shape, 1)
    taken = (row == 0) & (lane < 2)
    for q in range(per):
        run_near = jnp.zeros(shape, F32)
        run_far = run_near
        for i in range(count):
            low = in_ref[i, q, 1].astype(F32)
            dist_mid = jnp.broadcast_to(low[0:1, 0:1], shape)
            inv_mid = jnp.broadcast_to(low[0:1, 1:2], shape)
            high, rest = split(run_near - run_far * inv_mid)
            out_ref[i, q, 0] = high
            out_ref[i, q, 1] = rest
            out_ref[i, q, 2] = run_far.astype(BF16)
            if i < count - 1:
                total = in_ref[i, q, 0].astype(F32) + jnp.where(taken, 0.0, low)
                run_near = run_near + total
                run_far = run_far + (dist_mid * total + in_ref[i, q, 2].astype(F32))


def local_kernel(weight_ref, dist_ref, source_ref, pot_ref, edge_ref, plus_ref, minus_ref, cross_ref, lens):
    planes, height = pot_ref.shape[0], pot_ref.shape[1]
    chunks = plus_ref.shape[1]
    dist, near = weights(weight_ref, dist_ref, (SUB, LANES))
    far = [n * d for n, d in zip(near, dist)]
    inv, _ = inverses(source_ref, (SUB, LANES))

    def build(c, carry):
        for source, at in ((edge_ref, 0), (pot_ref, SUB)):
            for k in range(0, source.shape[1], 2 * SUB):
                size = min(2 * SUB, source.shape[1])
                fields = [source[s, k : k + size, columns(c)].astype(F32) for s in range(planes)]
                for t in range(0, size, SUB):
                    run_near = run_far = None
                    for s in range(planes):
                        field = fields[s][t : t + SUB]
                        run_near = near[s] * field if s == 0 else run_near + near[s] * field
                        run_far = far[s] * field if s == 0 else run_far + far[s] * field
                        lens[s, c, at + k + t : at + k + t + SUB] = run_near - run_far * inv[s]
        return carry

    lax.fori_loop(0, chunks, build, 0, unroll=4)
    row, lane = iotas()

    def sten(c, carry):
        before = lax.rem(c + chunks - 1, chunks)
        after = lax.rem(c + 1, chunks)
        for s in range(planes):
            here, firsts, seconds = [], [], []
            for at in range(0, SUB + height, SUB):
                mid = lens[s, c, at : at + SUB]
                first, second = along_x(lens[s, before, at : at + SUB], mid, lens[s, after, at : at + SUB], lane)
                here.append(mid)
                firsts.append(first)
                seconds.append(second)
            ys = shifts_y(here[1:], here[0], row)
            cs = shifts_y(firsts[1:], firsts[0], row)
            for k in range(height // SUB):
                at = slice(k * SUB, (k + 1) * SUB)
                sy = second_y(*ys[k])
                plus_ref[s, c, at] = (seconds[k + 1] + sy) - 60.0 * here[k + 1]
                minus_ref[s, c, at] = seconds[k + 1] - sy
                cross_ref[s, c, at] = first_y(*cs[k])
        return carry

    lax.fori_loop(0, chunks, sten, 0, unroll=2)


def field_of(ref, c, which, at, size):
    if which == 1:
        return ref[c, 2, at : at + size].astype(F32)
    return ref[c, 0, at : at + size].astype(F32) + ref[c, 1, at : at + size].astype(F32)


def own_kernel(pre_ref, out_ref, field):
    chunks, height = pre_ref.shape[0], pre_ref.shape[2]

    def build(c, carry):
        for f in range(2):
            field[f, c] = field_of(pre_ref, c, f, 0, height)
        return carry

    lax.fori_loop(0, chunks, build, 0, unroll=2)
    row, lane = iotas()
    zero = jnp.zeros((SUB, LANES), F32)

    def sten(c, carry):
        before = lax.rem(c + chunks - 1, chunks)
        after = lax.rem(c + 1, chunks)
        for f in range(2):
            here, firsts, seconds = [], [], []
            for at in range(0, height, SUB):
                mid = field[f, c, at : at + SUB]
                first, second = along_x(field[f, before, at : at + SUB], mid, field[f, after, at : at + SUB], lane)
                here.append(mid)
                firsts.append(first)
                seconds.append(second)
            ys = shifts_y(here, zero, row)
            cs = shifts_y(firsts, zero, row)
            for k in range(height // SUB):
                at = slice(k * SUB, (k + 1) * SUB)
                sy = second_y(*ys[k])
                out_ref[f, 0, c, at] = (seconds[k] + sy) - 60.0 * here[k]
                out_ref[f, 1, c, at] = seconds[k] - sy
                out_ref[f, 2, c, at] = first_y(*cs[k])
        return carry

    lax.fori_loop(0, chunks, sten, 0, unroll=4)


def join_kernel(source_ref, edge_ref, own_ref, plus_ref, minus_ref, cross_ref, conv_ref, one_ref, two_ref, field):
    planes, chunks, height = plus_ref.shape[0], plus_ref.shape[1], plus_ref.shape[2]
    per = chunks // STEPS
    base = pl.program_id(0) * per
    inv, inv_mid = inverses(source_ref, (SUB, LANES))
    slope = [inv_mid - v for v in inv]
    row, lane = iotas()
    tiles = height // SUB

    @pl.when(pl.program_id(0) == 0)
    def _():
        def build(c, carry):
            for f in range(2):
                field[f, c] = field_of(edge_ref, c, f, 0, SUB)
            return carry

        lax.fori_loop(0, chunks, build, 0, unroll=2)

    def sten(i, carry):
        c = base + i
        before = lax.rem(c + chunks - 1, chunks)
        after = lax.rem(c + 1, chunks)
        parts = []
        for f in range(2):
            here = field[f, c]
            first, _ = along_x(field[f, before], here, field[f, after], lane)

            def ends(value, near, far):
                d1 = jnp.where(row < 1, pltpu.roll(value, 1, 0), 0.0)
                d2 = jnp.where(row < 2, pltpu.roll(value, 2, 0), 0.0)
                u1 = jnp.where(row >= SUB - 1, pltpu.roll(value, SUB - 1, 0), 0.0)
                u2 = jnp.where(row >= SUB - 2, pltpu.roll(value, SUB - 2, 0), 0.0)
                return near * d1 - far * d2, abs(near) * u1 - abs(far) * u2

            sy = ends(here, 16.0, 1.0)
            cy = ends(first, -8.0, -1.0)
            field_parts = []
            for k in range(tiles):
                at = slice(k * SUB, (k + 1) * SUB)
                plus, minus, cross = (own_ref[f, n, c, at] for n in range(3))
                for edge, e in ((0, 0), (tiles - 1, 1)):
                    if k == edge:
                        plus, minus, cross = plus + sy[e], minus - sy[e], cross + cy[e]
                field_parts.append((plus, minus, cross))
            parts.append(field_parts)
        for s in range(planes):
            for ref, n, local, scale in (
                (conv_ref, 0, plus_ref, 1.0 / 24.0),
                (one_ref, 1, minus_ref, 1.0 / 24.0),
                (two_ref, 2, cross_ref, 1.0 / 144.0),
            ):
                rows = [
                    (local[s, c, k * SUB : (k + 1) * SUB] + parts[0][k][n] + slope[s] * parts[1][k][n]) * scale
                    for k in range(tiles)
                ]
                ref[s, :, columns(i)] = jnp.concatenate(rows, 0).astype(BF16)
        return carry

    lax.fori_loop(0, per, sten, 0, unroll=4)


def on_device(potentials, shell_weight, shell_dist, source_dist):
    shells, height, width = potentials.shape
    chunks = width // LANES
    count = lax.axis_size("los")
    sky = lax.axis_size("sky")
    forward = [(i, (i + 1) % sky) for i in range(sky)]
    backward = [((i + 1) % sky, i) for i in range(sky)]
    size = potentials.size

    pot_before = lax.ppermute(potentials[:, height - 2 :], "sky", forward)
    pot_after = lax.ppermute(potentials[:, :2], "sky", backward)
    pot_edge = jnp.concatenate([pot_after, jnp.zeros((shells, SUB - 4, width), BF16), pot_before], 1)

    piece = (3, height, LANES)
    totals = pl.pallas_call(
        totals_kernel,
        out_shape=jax.ShapeDtypeStruct((chunks,) + piece, BF16),
        in_specs=[SMEM, SMEM, SMEM, VMEM],
        out_specs=VMEM,
        compiler_params=params(),
        cost_estimate=cost(4 * size, 6 * size),
    )(shell_weight, shell_dist, source_dist, potentials)
    received = lax.all_to_all(totals, "los", split_axis=0, concat_axis=0, tiled=True)
    earlier = pl.pallas_call(
        earlier_kernel,
        out_shape=jax.ShapeDtypeStruct((count, chunks // count) + piece, BF16),
        in_specs=[VMEM],
        out_specs=VMEM,
        compiler_params=params(),
        cost_estimate=cost(4 * size, 6 * size),
    )(received.reshape((count, chunks // count) + piece))
    prefix = lax.all_to_all(earlier.reshape((chunks,) + piece), "los", split_axis=0, concat_axis=0, tiled=True)

    grids = [f32(shells, chunks, height, LANES)] * 3
    local = pl.pallas_call(
        local_kernel,
        out_shape=grids,
        in_specs=[SMEM, SMEM, SMEM, VMEM, VMEM],
        out_specs=[VMEM] * 3,
        scratch_shapes=[pltpu.VMEM((shells, chunks, height + SUB, LANES), F32)],
        compiler_params=params(),
        cost_estimate=cost(60 * size, 20 * size),
    )(shell_weight, shell_dist, source_dist, potentials, pot_edge)
    prefix, local = lax.optimization_barrier((prefix, local))

    pre_before = lax.ppermute(prefix[:, :, height - 2 :], "sky", forward)
    pre_after = lax.ppermute(prefix[:, :, :2], "sky", backward)
    own = pl.pallas_call(
        own_kernel,
        out_shape=f32(2, 3, chunks, height, LANES),
        in_specs=[VMEM],
        out_specs=VMEM,
        scratch_shapes=[pltpu.VMEM((2, chunks, height, LANES), F32)],
        compiler_params=params(),
        cost_estimate=cost(30 * size, 20 * size),
    )(prefix)
    pre_edge = jnp.concatenate([pre_after, jnp.zeros((chunks, 3, SUB - 4, LANES), BF16), pre_before], 2)

    block = pl.BlockSpec((shells, height, width // STEPS), lambda i: (0, 0, i))
    return tuple(
        pl.pallas_call(
            join_kernel,
            grid=(STEPS,),
            out_shape=[jax.ShapeDtypeStruct(potentials.shape, BF16)] * 3,
            in_specs=[SMEM] + [VMEM] * 5,
            out_specs=[block] * 3,
            scratch_shapes=[pltpu.VMEM((2, chunks, SUB, LANES), F32)],
            compiler_params=params(),
            cost_estimate=cost(40 * size, 20 * size),
        )(source_dist, pre_edge, own, *local)
    )


def solution(mesh):
    return jax.shard_map(
        on_device,
        mesh=mesh,
        in_specs=(P("los", "sky", None), P("los"), P("los"), P("los")),
        out_specs=(P("los", "sky", None), P("los", "sky", None), P("los", "sky", None)),
        check_vma=False,
    )
```

time: 67.3 us -> 60.5 us (0.90)
  the two profiles are of different devices: /device:TPU:1 before, /device:TPU:32 now
where the time goes in v2:
time: 60.5 us; the launch traced here: 60.1 us
  waiting for transfers between devices  25.3 us (42%)
  starting transfers between devices  18.5 us (31%)
  Pallas kernels  10.9 us (18%)
  local copies, waits for them, and re-layouts  4.27 us (7%)
  between operations  0.76 us (1%)
    all_to_all x1, waiting for transfers between devices, on_device(): lax.all_to_all(totals, 'los', split_axis=0, concat_axis=0, tiled=True)  12.8 us
    all_to_all x1, starting transfers between devices, on_device(): lax.all_to_all(totals, 'los', split_axis=0, concat_axis=0, tiled=True)  11.3 us
    all_to_all x1, waiting for transfers between devices, on_device(): lax.all_to_all(earlier.reshape((chunks,) + piece), 'los', split_axis=0, c...  9.38 us
    all_to_all x1, starting transfers between devices, on_device(): lax.all_to_all(earlier.reshape((chunks,) + piece), 'los', split_axis=0, c...  4.78 us
    unnamed x20, local copies, waits for them, and re-layouts  4 us
    pallas_call x1, Pallas kernels, on_device(): pl.pallas_call(local_kernel, out_shape=grids, in_specs=[SMEM, SMEM, SMEM,...  3.86 us
    pallas_call x1, Pallas kernels, on_device(): pl.pallas_call(join_kernel, grid=(STEPS,), out_shape=[jax.ShapeDtypeStruc...  3.24 us
    ppermute x1, waiting for transfers between devices, on_device(): pre_before = lax.ppermute(prefix[:, :, height - 2:], 'sky', forward)  2.97 us
  transfers between devices with their start and end apart: 6, of which 4 were waited for; matrix products, arithmetic and copies ran while one was open for 1% of the time, Pallas kernels for 10%

profile of v2, /device:TPU:32, one launch (start us, length us, event | category | flops | bytes accessed | tf_op | source)
XLA Modules:
  0.0 60.1 jit_solution(15913482404693034982)
XLA Ops:
  0.6 0.0 copy-start
  0.6 1.0 %copy-done = bf16[4,16,4096]{2,1,0:T(8,128)(2,1)S(1)} copy-done((bf16[4,16,4096]{2,1,0:T(8,128)(2,1)S(1)}, bf16[4,16,4096]{2,1,0:T(8,128)(2,1)}, u32[]{:S(2)}) %copy-start) | copy-done | bytes 524312
  1.7 0.7 %copy-done.4 = f32[4]{0:T(128)S(1)} copy-done((f32[4]{0:T(128)S(1)}, f32[4]{0:T(128)}, u32[]{:S(2)}) %copy-start.4) | copy-done | bytes 40
  2.3 0.7 %copy-done.6 = f32[4]{0:T(128)S(1)} copy-done((f32[4]{0:T(128)S(1)}, f32[4]{0:T(128)}, u32[]{:S(2)}) %copy-start.6) | copy-done | bytes 40
  3.0 0.7 %copy-done.8 = f32[4]{0:T(128)S(1)} copy-done((f32[4]{0:T(128)S(1)}, f32[4]{0:T(128)}, u32[]{:S(2)}) %copy-start.8) | copy-done | bytes 40
  3.6 1.6 %shard_map.67 = bf16[32,3,16,128]{3,2,1,0:T(8,128)(2,1)} custom-call(f32[4]{0:T(128)S(1)} %copy-done.6, f32[4]{0:T(128)S(1)} %copy-done.8, f32[4]{0:T(128)S(1)} %copy-done.4, bf16[4,16,4096]{2,1,0:T(8,128)(2,1)S(1)} %copy-done), custom_call_target="tpu_custom_call" | custom-call | flops 1048576 | bytes 1572864 | tf_op jit(solution)/shard_map/pallas_call | solution.py:311
  5.2 11.3 %all-to-all-start = ((bf16[32,3,16,128]{3,2,1,0:T(8,128)(2,1)}), bf16[32,3,16,128]{3,2,1,0:T(8,128)(2,1)S(1)}, u32[]{:S(2)}, u32[]{:S(2)}) async-start(bf16[32,3,16,128]{3,2,1,0:T(8,128)(2,1)} %shard_map.67), calls=%async_computation | async-start | bytes 786432 | tf_op jit(solution)/shard_map/all_to_all | solution.py:319
  16.5 0.0 copy-done.1
  16.5 0.1 fusion
  16.7 1.9 %collective-permute-start = (bf16[4,2,4096]{2,1,0:T(2,128)(2,1)S(1)}, bf16[4,2,4096]{2,1,0:T(2,128)(2,1)S(1)}, u32[]{:S(2)}, u32[]{:S(2)}) collective-permute-start(bf16[4,2,4096]{2,1,0:T(2,128)(2,1)S(1)} %get-tuple-element.17), channel_id=1, source_target_pairs={{1,0},{2,1},{3,2},{4,3},{5,4},{6,5},{7,6},{0,7},{9,8},{10,9},{11,1... | collective-permute-start | bytes 196616 | tf_op jit(solution)/shard_map/ppermute | solution.py:307
  18.6 0.0 collective-permute-start.1
  18.6 0.1 pad.4.clone
  18.7 12.8 %all-to-all-done = bf16[32,3,16,128]{3,2,1,0:T(8,128)(2,1)S(1)} async-done(((bf16[32,3,16,128]{3,2,1,0:T(8,128)(2,1)}), bf16[32,3,16,128]{3,2,1,0:T(8,128)(2,1)S(1)}, u32[]{:S(2)}, u32[]{:S(2)}) %all-to-all-start) | async-done | bytes 393248 | tf_op jit(solution)/shard_map/all_to_all | solution.py:319
  31.4 1.0 %shard_map.68 = bf16[32,1,3,16,128]{4,3,2,1,0:T(8,128)(2,1)} custom-call(bf16[32,1,3,16,128]{4,3,2,1,0:T(8,128)(2,1)S(1)} %bitcast.2), custom_call_target="tpu_custom_call" | custom-call | flops 1048576 | bytes 1572864 | tf_op jit(solution)/shard_map/pallas_call | solution.py:320
  32.4 4.8 %all-to-all-start.1 = ((bf16[32,3,16,128]{3,2,1,0:T(8,128)(2,1)}), bf16[32,3,16,128]{3,2,1,0:T(8,128)(2,1)S(1)}, u32[]{:S(2)}, u32[]{:S(2)}) async-start(bf16[32,3,16,128]{3,2,1,0:T(8,128)(2,1)} %bitcast.1), calls=%async_computation.1 | async-start | bytes 786432 | tf_op jit(solution)/shard_map/all_to_all | solution.py:328
  37.2 0.0 collective-permute-done
  37.2 0.0 collective-permute-done.1
  37.2 0.2 pad_maximum_fusion.edge_ref
  37.3 0.0 copy-done.5
  37.4 0.0 copy-done.7
  37.4 0.0 copy-done.9
  37.4 3.9 %shard_map.69 = (f32[4,32,16,128]{3,2,1,0:T(8,128)S(1)}, f32[4,32,16,128]{3,2,1,0:T(8,128)S(1)}, f32[4,32,16,128]{3,2,1,0:T(8,128)S(1)}) custom-call(f32[4]{0:T(128)S(1)} %copy-done.7, f32[4]{0:T(128)S(1)} %copy-done.9, f32[4]{0:T(128)S(1)} %copy-done.5, bf16[4,16,4096]{2,1,0:T(8,128)(2,1)S(1)} %copy-done.1, bf16[4,8,4096]{2,1,0:T(8,128)(2,1)S(1)} %pad_maximum_fusion.edge_ref), custom_call_target="tpu_custom_call" | custom-call | flops 15728640 | bytes 5242880 | tf_op jit(solution)/shard_map/pallas_call | solution.py:331
  41.3 1.0 %copy-done.2 = f32[4,32,16,128]{3,2,1,0:T(8,128)} copy-done((f32[4,32,16,128]{3,2,1,0:T(8,128)}, f32[4,32,16,128]{3,2,1,0:T(8,128)S(1)}, u32[]{:S(2)}) %copy-start.2) | copy-done | bytes 1048600
  42.2 9.4 %all-to-all-done.1.pre_ref = bf16[32,3,16,128]{3,2,1,0:T(8,128)(2,1)S(1)} async-done(((bf16[32,3,16,128]{3,2,1,0:T(8,128)(2,1)}), bf16[32,3,16,128]{3,2,1,0:T(8,128)(2,1)S(1)}, u32[]{:S(2)}, u32[]{:S(2)}) %all-to-all-start.1) | async-done | bytes 393248 | tf_op jit(solution)/shard_map/all_to_all | solution.py:328
  51.6 0.1 fusion.1
  51.7 0.3 collective-permute-start.2
  52.0 0.2 collective-permute-start.3
  52.2 1.3 %shard_map.70.own_ref = f32[2,3,32,16,128]{4,3,2,1,0:T(8,128)S(1)} custom-call(bf16[32,3,16,128]{3,2,1,0:T(8,128)(2,1)S(1)} %all-to-all-done.1.pre_ref), custom_call_target="tpu_custom_call" | custom-call | flops 7864320 | bytes 5242880 | tf_op jit(solution)/shard_map/pallas_call | solution.py:344
  53.5 0.2 collective-permute-done.2
  53.8 3.0 %collective-permute-done.3 = bf16[32,3,2,128]{3,2,1,0:T(2,128)(2,1)S(1)} collective-permute-done((bf16[32,3,2,128]{3,2,1,0:T(2,128)(2,1)S(1)}, bf16[32,3,2,128]{3,2,1,0:T(2,128)(2,1)S(1)}, u32[]{:S(2)}, u32[]{:S(2)}) %collective-permute-start.3) | collective-permute-done | bytes 49184 | tf_op jit(solution)/shard_map/ppermute | solution.py:342
  56.7 0.1 pad_maximum_fusion.1.edge_ref
  56.9 3.2 %shard_map.71 = (bf16[4,16,4096]{2,1,0:T(8,128)(2,1)}, bf16[4,16,4096]{2,1,0:T(8,128)(2,1)}, bf16[4,16,4096]{2,1,0:T(8,128)(2,1)}) custom-call(f32[4]{0:T(128)S(1)} %copy-done.5, bf16[32,3,8,128]{3,2,1,0:T(8,128)(2,1)S(1)} %pad_maximum_fusion.1.edge_ref, f32[2,3,32,16,128]{4,3,2,1,0:T(8,128)S(1)} %shard_map.70.own_ref, ...), custom_call_target="tpu_custom_call" | custom-call | flops 10485760 | bytes 5242880 | tf_op jit(solution)/shard_map/pallas_call | solution.py:357
  (11 shorter events, 0.0 us)
Async XLA Ops:
  0.6 1.0 %copy-start = (bf16[4,16,4096]{2,1,0:T(8,128)(2,1)S(1)}, bf16[4,16,4096]{2,1,0:T(8,128)(2,1)}, u32[]{:S(2)}) copy-start(bf16[4,16,4096]{2,1,0:T(8,128)(2,1)} %pot_ref.3) | copy-start | bytes 1572868
  1.7 0.7 %copy-start.4 = (f32[4]{0:T(128)S(1)}, f32[4]{0:T(128)}, u32[]{:S(2)}) copy-start(f32[4]{0:T(128)} %source_ref.5) | copy-start | bytes 52
  2.3 0.7 %copy-start.6 = (f32[4]{0:T(128)S(1)}, f32[4]{0:T(128)}, u32[]{:S(2)}) copy-start(f32[4]{0:T(128)} %weight_ref.3) | copy-start | bytes 52
  3.0 0.7 %copy-start.8 = (f32[4]{0:T(128)S(1)}, f32[4]{0:T(128)}, u32[]{:S(2)}) copy-start(f32[4]{0:T(128)} %dist_ref.3) | copy-start | bytes 52
  3.6 12.9 %copy-start.1 = (bf16[4,16,4096]{2,1,0:T(8,128)(2,1)S(1)}, bf16[4,16,4096]{2,1,0:T(8,128)(2,1)}, u32[]{:S(2)}) copy-start(bf16[4,16,4096]{2,1,0:T(8,128)(2,1)} %pot_ref.3) | copy-start | bytes 1572868
  5.2 32.1 %copy-start.5 = (f32[4]{0:T(128)S(1)}, f32[4]{0:T(128)}, u32[]{:S(2)}) copy-start(f32[4]{0:T(128)} %source_ref.5) | copy-start | bytes 52
  5.2 32.1 %copy-start.7 = (f32[4]{0:T(128)S(1)}, f32[4]{0:T(128)}, u32[]{:S(2)}) copy-start(f32[4]{0:T(128)} %weight_ref.3) | copy-start | bytes 52
  5.2 32.2 %copy-start.9 = (f32[4]{0:T(128)S(1)}, f32[4]{0:T(128)}, u32[]{:S(2)}) copy-start(f32[4]{0:T(128)} %dist_ref.3) | copy-start | bytes 52
  5.2 26.2 %all-to-all-start = ((bf16[32,3,16,128]{3,2,1,0:T(8,128)(2,1)}), bf16[32,3,16,128]{3,2,1,0:T(8,128)(2,1)S(1)}, u32[]{:S(2)}, u32[]{:S(2)}) async-start(bf16[32,3,16,128]{3,2,1,0:T(8,128)(2,1)} %shard_map.67), calls=%async_computation | async-start | bytes 786432 | tf_op jit(solution)/shard_map/all_to_all | solution.py:319
  16.7 20.5 %collective-permute-start = (bf16[4,2,4096]{2,1,0:T(2,128)(2,1)S(1)}, bf16[4,2,4096]{2,1,0:T(2,128)(2,1)S(1)}, u32[]{:S(2)}, u32[]{:S(2)}) collective-permute-start(bf16[4,2,4096]{2,1,0:T(2,128)(2,1)S(1)} %get-tuple-element.17), channel_id=1, source_target_pairs={{1,0},{2,1},{3,2},{4,3},{5,4},{6,5},{7,6},{0,7},{9,8},{10,9},{11,1... | collective-permute-start | bytes 196616 | tf_op jit(solution)/shard_map/ppermute | solution.py:307
  18.6 18.6 %collective-permute-start.1 = (bf16[4,2,4096]{2,1,0:T(2,128)(2,1)S(1)}, bf16[4,2,4096]{2,1,0:T(2,128)(2,1)S(1)}, u32[]{:S(2)}, u32[]{:S(2)}) collective-permute-start(bf16[4,2,4096]{2,1,0:T(2,128)(2,1)S(1)} %get-tuple-element.18), channel_id=1, source_target_pairs={{0,1},{1,2},{2,3},{3,4},{4,5},{5,6},{6,7},{7,0},{8,9},{9,10},{10,1... | collective-permute-start | bytes 196616 | tf_op jit(solution)/shard_map/ppermute | solution.py:306
  32.4 19.3 %all-to-all-start.1 = ((bf16[32,3,16,128]{3,2,1,0:T(8,128)(2,1)}), bf16[32,3,16,128]{3,2,1,0:T(8,128)(2,1)S(1)}, u32[]{:S(2)}, u32[]{:S(2)}) async-start(bf16[32,3,16,128]{3,2,1,0:T(8,128)(2,1)} %bitcast.1), calls=%async_computation.1 | async-start | bytes 786432 | tf_op jit(solution)/shard_map/all_to_all | solution.py:328
  41.2 1.0 %copy-start.2 = (f32[4,32,16,128]{3,2,1,0:T(8,128)}, f32[4,32,16,128]{3,2,1,0:T(8,128)S(1)}, u32[]{:S(2)}) copy-start(f32[4,32,16,128]{3,2,1,0:T(8,128)S(1)} %get-tuple-element.16.cross_ref) | copy-start | bytes 3145732
  51.6 5.3 %copy-start.3 = (f32[4,32,16,128]{3,2,1,0:T(8,128)S(1)}, f32[4,32,16,128]{3,2,1,0:T(8,128)}, u32[]{:S(2)}) copy-start(f32[4,32,16,128]{3,2,1,0:T(8,128)} %copy-done.2) | copy-start | bytes 3145732
  51.7 2.1 %collective-permute-start.2 = (bf16[32,3,2,128]{3,2,1,0:T(2,128)(2,1)S(1)}, bf16[32,3,2,128]{3,2,1,0:T(2,128)(2,1)S(1)}, u32[]{:S(2)}, u32[]{:S(2)}) collective-permute-start(bf16[32,3,2,128]{3,2,1,0:T(2,128)(2,1)S(1)} %get-tuple-element.19), channel_id=1, source_target_pairs={{1,0},{2,1},{3,2},{4,3},{5,4},{6,5},{7,6},{0,7},{9,8},{10,9},{11,1... | collective-permute-start | bytes 147464 | tf_op jit(solution)/shard_map/ppermute | solution.py:343
  52.0 4.7 %collective-permute-start.3 = (bf16[32,3,2,128]{3,2,1,0:T(2,128)(2,1)S(1)}, bf16[32,3,2,128]{3,2,1,0:T(2,128)(2,1)S(1)}, u32[]{:S(2)}, u32[]{:S(2)}) collective-permute-start(bf16[32,3,2,128]{3,2,1,0:T(2,128)(2,1)S(1)} %get-tuple-element.20), channel_id=1, source_target_pairs={{0,1},{1,2},{2,3},{3,4},{4,5},{5,6},{6,7},{7,0},{8,9},{9,10},{10,1... | collective-permute-start | bytes 147464 | tf_op jit(solution)/shard_map/ppermute | solution.py:342

commit v3 on v2

--- a/solution.py
+++ b/solution.py
@@ -10,13 +10,16 @@
 LANES = 128
 SUB = 8
 STEPS = 4
+SCALE = 1.0 / 24.0
+SCALE_CROSS = 1.0 / 144.0
 VMEM = pl.BlockSpec(memory_space=pltpu.VMEM)
+ANY = pl.BlockSpec(memory_space=pl.ANY)
 SMEM = pl.BlockSpec(memory_space=pltpu.SMEM)
 F32 = jnp.float32
 BF16 = jnp.bfloat16
 
 
-def params(mib=24):
+def params(mib=12):
     return pltpu.CompilerParams(vmem_limit_bytes=mib * 1024 * 1024)
 
 
@@ -92,8 +95,28 @@
     return value.astype(BF16).astype(F32)
 
 
-def totals_kernel(weight_ref, dist_ref, source_ref, pot_ref, out_ref):
-    shells, height = pot_ref.shape[0], pot_ref.shape[1]
+def totals_kernel(weight_hbm, dist_hbm, source_hbm, pot_hbm, out_hbm, pot, out, weight_ref, dist_ref, source_ref,
+                  small_sems, in_sems, out_sems):
+    shells, height = pot.shape[0], pot.shape[1]
+    chunks = out.shape[0]
+    per = chunks // STEPS
+    small = [
+        pltpu.make_async_copy(src, dst, small_sems.at[k])
+        for k, (src, dst) in enumerate(((weight_hbm, weight_ref), (dist_hbm, dist_ref), (source_hbm, source_ref)))
+    ]
+    pieces = [pl.ds(i * per * LANES, per * LANES) for i in range(STEPS)]
+    loads = [
+        pltpu.make_async_copy(pot_hbm.at[:, :, piece], pot.at[:, :, piece], in_sems.at[i])
+        for i, piece in enumerate(pieces)
+    ]
+    stores = [
+        pltpu.make_async_copy(out.at[pl.ds(i * per, per)], out_hbm.at[pl.ds(i * per, per)], out_sems.at[i])
+        for i in range(STEPS)
+    ]
+    for copy in small + loads:
+        copy.start()
+    for copy in small:
+        copy.wait()
     shape = (height, LANES)
     dist, near = weights(weight_ref, dist_ref, shape)
     dist_mid = rounded(0.5 * (dist[0] + dist[-1]))
@@ -104,20 +127,27 @@
     first = (row == 0) & (lane == 0)
     second = (row == 0) & (lane == 1)
 
-    def one(c, carry):
-        total_near = total_off = None
-        for j in range(shells):
-            field = pot_ref[j, :, columns(c)].astype(F32)
-            total_near = near[j] * field if j == 0 else total_near + near[j] * field
-            total_off = off[j] * field if j == 0 else total_off + off[j] * field
-        high = total_near.astype(BF16)
-        low = total_near - high.astype(F32)
-        out_ref[c, 0] = high
-        out_ref[c, 1] = jnp.where(first, dist_mid, jnp.where(second, inv_mid, low)).astype(BF16)
-        out_ref[c, 2] = total_off.astype(BF16)
-        return carry
-
-    lax.fori_loop(0, out_ref.shape[0], one, 0, unroll=4)
+    for i in range(STEPS):
+        loads[i].wait()
+
+        def one(k, carry):
+            c = i * per + k
+            total_near = total_off = None
+            for j in range(shells):
+                field = pot[j, :, columns(c)].astype(F32)
+                total_near = near[j] * field if j == 0 else total_near + near[j] * field
+                total_off = off[j] * field if j == 0 else total_off + off[j] * field
+            high = total_near.astype(BF16)
+            low = total_near - high.astype(F32)
+            out[c, 0] = high
+            out[c, 1] = jnp.where(first, dist_mid, jnp.where(second, inv_mid, low)).astype(BF16)
+            out[c, 2] = total_off.astype(BF16)
+            return carry
+
+        lax.fori_loop(0, per, one, 0, unroll=4)
+        stores[i].start()
+    for copy in stores:
+        copy.wait()
 
 
 def earlier_kernel(in_ref, out_ref):
@@ -143,9 +173,9 @@
                 run_far = run_far + (dist_mid * total + in_ref[i, q, 2].astype(F32))
 
 
-def local_kernel(weight_ref, dist_ref, source_ref, pot_ref, edge_ref, plus_ref, minus_ref, cross_ref, lens):
+def local_kernel(weight_ref, dist_ref, source_ref, pot_ref, edge_ref, out_ref, lens):
     planes, height = pot_ref.shape[0], pot_ref.shape[1]
-    chunks = plus_ref.shape[1]
+    chunks = out_ref.shape[2]
     dist, near = weights(weight_ref, dist_ref, (SUB, LANES))
     far = [n * d for n, d in zip(near, dist)]
     inv, _ = inverses(source_ref, (SUB, LANES))
@@ -183,9 +213,9 @@
             for k in range(height // SUB):
                 at = slice(k * SUB, (k + 1) * SUB)
                 sy = second_y(*ys[k])
-                plus_ref[s, c, at] = (seconds[k + 1] + sy) - 60.0 * here[k + 1]
-                minus_ref[s, c, at] = seconds[k + 1] - sy
-                cross_ref[s, c, at] = first_y(*cs[k])
+                out_ref[s, 0, c, at] = (seconds[k + 1] + sy) - 60.0 * here[k + 1]
+                out_ref[s, 1, c, at] = seconds[k + 1] - sy
+                out_ref[s, 2, c, at] = first_y(*cs[k])
         return carry
 
     lax.fori_loop(0, chunks, sten, 0, unroll=2)
@@ -197,21 +227,25 @@
     return ref[c, 0, at : at + size].astype(F32) + ref[c, 1, at : at + size].astype(F32)
 
 
-def own_kernel(pre_ref, out_ref, field):
+def own_kernel(source_ref, pre_ref, local_ref, out_ref, field):
     chunks, height = pre_ref.shape[0], pre_ref.shape[2]
+    planes = local_ref.shape[0]
+    inv, inv_mid = inverses(source_ref, (SUB, LANES))
+    slope = [inv_mid - v for v in inv]
 
     def build(c, carry):
         for f in range(2):
             field[f, c] = field_of(pre_ref, c, f, 0, height)
         return carry
 
-    lax.fori_loop(0, chunks, build, 0, unroll=2)
+    lax.fori_loop(0, chunks, build, 0, unroll=4)
     row, lane = iotas()
     zero = jnp.zeros((SUB, LANES), F32)
 
     def sten(c, carry):
         before = lax.rem(c + chunks - 1, chunks)
         after = lax.rem(c + 1, chunks)
+        parts = []
         for f in range(2):
             here, firsts, seconds = [], [], []
             for at in range(0, height, SUB):
@@ -223,75 +257,74 @@
             ys = shifts_y(here, zero, row)
             cs = shifts_y(firsts, zero, row)
             for k in range(height // SUB):
-                at = slice(k * SUB, (k + 1) * SUB)
                 sy = second_y(*ys[k])
-                out_ref[f, 0, c, at] = (seconds[k] + sy) - 60.0 * here[k]
-                out_ref[f, 1, c, at] = seconds[k] - sy
-                out_ref[f, 2, c, at] = first_y(*cs[k])
-        return carry
-
-    lax.fori_loop(0, chunks, sten, 0, unroll=4)
-
-
-def join_kernel(source_ref, edge_ref, own_ref, plus_ref, minus_ref, cross_ref, conv_ref, one_ref, two_ref, field):
-    planes, chunks, height = plus_ref.shape[0], plus_ref.shape[1], plus_ref.shape[2]
+                parts.append(((seconds[k] + sy) - 60.0 * here[k], seconds[k] - sy, first_y(*cs[k])))
+        for k in range(height // SUB):
+            at = slice(k * SUB, (k + 1) * SUB)
+            for n, scale in enumerate((SCALE, SCALE, SCALE_CROSS)):
+                lens, far = parts[k][n], parts[height // SUB + k][n]
+                for s in range(planes):
+                    out_ref[s, n, c, at] = (local_ref[s, n, c, at] + lens + slope[s] * far) * scale
+        return carry
+
+    lax.fori_loop(0, chunks, sten, 0, unroll=2)
+
+
+def join_kernel(source_ref, edge_ref, own_ref, conv_hbm, one_hbm, two_hbm, conv_ref, one_ref, two_ref, field, sems):
+    planes, chunks, height = own_ref.shape[0], own_ref.shape[2], own_ref.shape[3]
     per = chunks // STEPS
-    base = pl.program_id(0) * per
     inv, inv_mid = inverses(source_ref, (SUB, LANES))
     slope = [inv_mid - v for v in inv]
     row, lane = iotas()
     tiles = height // SUB
 
-    @pl.when(pl.program_id(0) == 0)
-    def _():
-        def build(c, carry):
-            for f in range(2):
-                field[f, c] = field_of(edge_ref, c, f, 0, SUB)
-            return carry
-
-        lax.fori_loop(0, chunks, build, 0, unroll=2)
-
-    def sten(i, carry):
-        c = base + i
+    def build(c, carry):
+        for f in range(2):
+            field[f, c] = field_of(edge_ref, c, f, 0, SUB)
+        return carry
+
+    lax.fori_loop(0, chunks, build, 0, unroll=8)
+
+    def ends(value, near, far, sign):
+        d1 = jnp.where(row < 1, near * pltpu.roll(value, 1, 0), 0.0)
+        d2 = jnp.where(row < 2, far * pltpu.roll(value, 2, 0), 0.0)
+        u1 = jnp.where(row >= SUB - 1, near * pltpu.roll(value, SUB - 1, 0), 0.0)
+        u2 = jnp.where(row >= SUB - 2, far * pltpu.roll(value, SUB - 2, 0), 0.0)
+        return sign * (d1 - d2), u1 - u2
+
+    def sten(c, carry):
         before = lax.rem(c + chunks - 1, chunks)
         after = lax.rem(c + 1, chunks)
-        parts = []
+        ys, cs = [], []
         for f in range(2):
             here = field[f, c]
             first, _ = along_x(field[f, before], here, field[f, after], lane)
-
-            def ends(value, near, far):
-                d1 = jnp.where(row < 1, pltpu.roll(value, 1, 0), 0.0)
-                d2 = jnp.where(row < 2, pltpu.roll(value, 2, 0), 0.0)
-                u1 = jnp.where(row >= SUB - 1, pltpu.roll(value, SUB - 1, 0), 0.0)
-                u2 = jnp.where(row >= SUB - 2, pltpu.roll(value, SUB - 2, 0), 0.0)
-                return near * d1 - far * d2, abs(near) * u1 - abs(far) * u2
-
-            sy = ends(here, 16.0, 1.0)
-            cy = ends(first, -8.0, -1.0)
-            field_parts = []
-            for k in range(tiles):
-                at = slice(k * SUB, (k + 1) * SUB)
-                plus, minus, cross = (own_ref[f, n, c, at] for n in range(3))
-                for edge, e in ((0, 0), (tiles - 1, 1)):
-                    if k == edge:
-                        plus, minus, cross = plus + sy[e], minus - sy[e], cross + cy[e]
-                field_parts.append((plus, minus, cross))
-            parts.append(field_parts)
+            ys.append(ends(here, 16.0 * SCALE, SCALE, 1.0))
+            cs.append(ends(first, 8.0 * SCALE_CROSS, SCALE_CROSS, -1.0))
         for s in range(planes):
-            for ref, n, local, scale in (
-                (conv_ref, 0, plus_ref, 1.0 / 24.0),
-                (one_ref, 1, minus_ref, 1.0 / 24.0),
-                (two_ref, 2, cross_ref, 1.0 / 144.0),
-            ):
-                rows = [
-                    (local[s, c, k * SUB : (k + 1) * SUB] + parts[0][k][n] + slope[s] * parts[1][k][n]) * scale
-                    for k in range(tiles)
-                ]
-                ref[s, :, columns(i)] = jnp.concatenate(rows, 0).astype(BF16)
-        return carry
-
-    lax.fori_loop(0, per, sten, 0, unroll=4)
+            sums = []
+            for pair in (ys, cs):
+                sums.append([pair[0][e] + slope[s] * pair[1][e] for e in range(2)])
+            for ref, n, add in ((conv_ref, 0, sums[0]), (one_ref, 1, sums[0]), (two_ref, 2, sums[1])):
+                rows = []
+                for k in range(tiles):
+                    value = own_ref[s, n, c, k * SUB : (k + 1) * SUB]
+                    for at, e in ((0, 0), (tiles - 1, 1)):
+                        if k == at:
+                            value = value - add[e] if n == 1 else value + add[e]
+                    rows.append(value)
+                ref[s, :, columns(c)] = jnp.concatenate(rows, 0).astype(BF16)
+        return carry
+
+    copies = []
+    for i in range(STEPS):
+        lax.fori_loop(i * per, (i + 1) * per, sten, 0, unroll=4)
+        piece = pl.ds(i * per * LANES, per * LANES)
+        for n, (ref, hbm) in enumerate(((conv_ref, conv_hbm), (one_ref, one_hbm), (two_ref, two_hbm))):
+            copies.append(pltpu.make_async_copy(ref.at[:, :, piece], hbm.at[:, :, piece], sems.at[n, i]))
+            copies[-1].start()
+    for copy in copies:
+        copy.wait()
 
 
 def on_device(potentials, shell_weight, shell_dist, source_dist):
@@ -311,9 +344,17 @@
     totals = pl.pallas_call(
         totals_kernel,
         out_shape=jax.ShapeDtypeStruct((chunks,) + piece, BF16),
-        in_specs=[SMEM, SMEM, SMEM, VMEM],
-        out_specs=VMEM,
-        compiler_params=params(),
+        in_specs=[ANY] * 4,
+        out_specs=ANY,
+        scratch_shapes=[
+            pltpu.VMEM(potentials.shape, BF16),
+            pltpu.VMEM((chunks,) + piece, BF16),
+            *[pltpu.SMEM((shells,), F32)] * 3,
+            pltpu.SemaphoreType.DMA((3,)),
+            pltpu.SemaphoreType.DMA((STEPS,)),
+            pltpu.SemaphoreType.DMA((STEPS,)),
+        ],
+        compiler_params=params(60),
         cost_estimate=cost(4 * size, 6 * size),
     )(shell_weight, shell_dist, source_dist, potentials)
     received = lax.all_to_all(totals, "los", split_axis=0, concat_axis=0, tiled=True)
@@ -327,12 +368,12 @@
     )(received.reshape((count, chunks // count) + piece))
     prefix = lax.all_to_all(earlier.reshape((chunks,) + piece), "los", split_axis=0, concat_axis=0, tiled=True)
 
-    grids = [f32(shells, chunks, height, LANES)] * 3
+    grids = f32(shells, 3, chunks, height, LANES)
     local = pl.pallas_call(
         local_kernel,
         out_shape=grids,
         in_specs=[SMEM, SMEM, SMEM, VMEM, VMEM],
-        out_specs=[VMEM] * 3,
+        out_specs=VMEM,
         scratch_shapes=[pltpu.VMEM((shells, chunks, height + SUB, LANES), F32)],
         compiler_params=params(),
         cost_estimate=cost(60 * size, 20 * size),
@@ -343,27 +384,29 @@
     pre_after = lax.ppermute(prefix[:, :, :2], "sky", backward)
     own = pl.pallas_call(
         own_kernel,
-        out_shape=f32(2, 3, chunks, height, LANES),
-        in_specs=[VMEM],
+        out_shape=grids,
+        in_specs=[SMEM] + [VMEM] * 2,
         out_specs=VMEM,
         scratch_shapes=[pltpu.VMEM((2, chunks, height, LANES), F32)],
         compiler_params=params(),
         cost_estimate=cost(30 * size, 20 * size),
-    )(prefix)
+    )(source_dist, prefix, local)
     pre_edge = jnp.concatenate([pre_after, jnp.zeros((chunks, 3, SUB - 4, LANES), BF16), pre_before], 2)
 
-    block = pl.BlockSpec((shells, height, width // STEPS), lambda i: (0, 0, i))
     return tuple(
         pl.pallas_call(
             join_kernel,
-            grid=(STEPS,),
             out_shape=[jax.ShapeDtypeStruct(potentials.shape, BF16)] * 3,
-            in_specs=[SMEM] + [VMEM] * 5,
-            out_specs=[block] * 3,
-            scratch_shapes=[pltpu.VMEM((2, chunks, SUB, LANES), F32)],
+            in_specs=[SMEM] + [VMEM] * 2,
+            out_specs=[ANY] * 3,
+            scratch_shapes=[
+                *[pltpu.VMEM(potentials.shape, BF16)] * 3,
+                pltpu.VMEM((2, chunks, SUB, LANES), F32),
+                pltpu.SemaphoreType.DMA((3, STEPS)),
+            ],
             compiler_params=params(),
             cost_estimate=cost(40 * size, 20 * size),
-        )(source_dist, pre_edge, own, *local)
+        )(source_dist, pre_edge, own)
     )
 
 

time: 60.5 us -> 57.2 us (0.945)
  waiting for transfers between devices: 25.3 us -> 22.6 us
  local copies, waits for them, and re-layouts: 4.27 us -> 2.35 us
  Pallas kernels: 10.9 us -> 12.2 us
    unnamed x20 -> x8, local copies, waits for them, and re-layouts: 4 us -> 1.05 us
    ppermute x1, waiting for transfers between devices: 2.97 us -> 1.58 us  [on_device(): pre_before = lax.ppermute(prefix[:, :, height - 2:], 'sky', forward)]
    slice x1, local copies, waits for them, and re-layouts: 0.11 us -> 1.14 us  [on_device(): pot_after = lax.ppermute(potentials[:, :2], 'sky', backward)]
    all_to_all x1, waiting for transfers between devices: 12.8 us -> 11.7 us  [on_device(): lax.all_to_all(totals, 'los', split_axis=0, concat_axis=0, tiled=True)]
    pallas_call x2, Pallas kernels: 4.54 us -> 5.43 us  [the longest x1 2.91 us: on_device(): pl.pallas_call(own_kernel, out_shape=grids, in_specs=[SMEM] + [VMEM] * 2,...]
  transfers between devices with their start and end apart: 6 -> 6, of which waited for: 4 -> 3; matrix products, arithmetic and copies ran while one was open for 1% -> 2% of each run, Pallas kernels for 10% -> 14%
where the time goes in v3:
time: 57.2 us; the launch traced here: 56.6 us
  waiting for transfers between devices  22.6 us (40%)
  starting transfers between devices  18.4 us (32%)
  Pallas kernels  12.2 us (21%)
  local copies, waits for them, and re-layouts  2.35 us (4%)
  between operations  0.77 us (1%)
    all_to_all x1, waiting for transfers between devices, on_device(): lax.all_to_all(totals, 'los', split_axis=0, concat_axis=0, tiled=True)  11.7 us
    all_to_all x1, starting transfers between devices, on_device(): lax.all_to_all(totals, 'los', split_axis=0, concat_axis=0, tiled=True)  11.2 us
    all_to_all x1, waiting for transfers between devices, on_device(): lax.all_to_all(earlier.reshape((chunks,) + piece), 'los', split_axis=0, c...  9.31 us
    all_to_all x1, starting transfers between devices, on_device(): lax.all_to_all(earlier.reshape((chunks,) + piece), 'los', split_axis=0, c...  4.78 us
    pallas_call x1, Pallas kernels, on_device(): pl.pallas_call(local_kernel, out_shape=grids, in_specs=[SMEM, SMEM, SMEM,...  3.88 us
    pallas_call x1, Pallas kernels, on_device(): pl.pallas_call(own_kernel, out_shape=grids, in_specs=[SMEM] + [VMEM] * 2,...  2.91 us
    pallas_call x1, Pallas kernels, on_device(): pl.pallas_call(join_kernel, out_shape=[jax.ShapeDtypeStruct(potentials.sh...  2.51 us
    pallas_call x1, Pallas kernels, on_device(): pl.pallas_call(totals_kernel, out_shape=jax.ShapeDtypeStruct((chunks,) +...  1.92 us
  transfers between devices with their start and end apart: 6, of which 3 were waited for; matrix products, arithmetic and copies ran while one was open for 2% of the time, Pallas kernels for 14%

profile of v3, /device:TPU:32, one launch (start us, length us, event | category | flops | bytes accessed | tf_op | source)
XLA Modules:
  0.0 56.6 jit_solution(5935767850772427509)
XLA Ops:
  0.6 0.0 copy-start.1
  0.6 0.0 copy-start.3
  0.7 0.0 copy-start.2
  0.7 1.9 %shard_map.67 = bf16[32,3,16,128]{3,2,1,0:T(8,128)(2,1)} custom-call(f32[4]{0:T(128)} %weight_ref.1, f32[4]{0:T(128)} %dist_ref.1, f32[4]{0:T(128)} %source_ref.5, bf16[4,16,4096]{2,1,0:T(8,128)(2,1)} %pot_ref.1), custom_call_target="tpu_custom_call" | custom-call | flops 1048576 | bytes 1572864 | tf_op jit(solution)/shard_map/pallas_call | solution.py:344
  2.6 11.2 %all-to-all-start = ((bf16[32,3,16,128]{3,2,1,0:T(8,128)(2,1)}), bf16[32,3,16,128]{3,2,1,0:T(8,128)(2,1)S(1)}, u32[]{:S(2)}, u32[]{:S(2)}) async-start(bf16[32,3,16,128]{3,2,1,0:T(8,128)(2,1)} %shard_map.67), calls=%async_computation | async-start | bytes 786432 | tf_op jit(solution)/shard_map/all_to_all | solution.py:360
  13.8 1.1 %fusion = (bf16[4,2,4096]{2,1,0:T(2,128)(2,1)S(1)}, bf16[4,2,4096]{2,1,0:T(2,128)(2,1)S(1)}) fusion(bf16[4,16,4096]{2,1,0:T(8,128)(2,1)} %pot_ref.1), kind=kLoop, calls=%fused_computation.2 | loop fusion | bytes 262144 | tf_op jit(solution)/shard_map/slice | solution.py:340
  14.9 1.9 %collective-permute-start = (bf16[4,2,4096]{2,1,0:T(2,128)(2,1)S(1)}, bf16[4,2,4096]{2,1,0:T(2,128)(2,1)S(1)}, u32[]{:S(2)}, u32[]{:S(2)}) collective-permute-start(bf16[4,2,4096]{2,1,0:T(2,128)(2,1)S(1)} %get-tuple-element.7), channel_id=1, source_target_pairs={{1,0},{2,1},{3,2},{4,3},{5,4},{6,5},{7,6},{0,7},{9,8},{10,9},{11,1... | collective-permute-start | bytes 196616 | tf_op jit(solution)/shard_map/ppermute | solution.py:340
  16.8 0.0 collective-permute-start.1
  16.8 0.1 pad.4.clone
  16.9 11.7 %all-to-all-done = bf16[32,3,16,128]{3,2,1,0:T(8,128)(2,1)S(1)} async-done(((bf16[32,3,16,128]{3,2,1,0:T(8,128)(2,1)}), bf16[32,3,16,128]{3,2,1,0:T(8,128)(2,1)S(1)}, u32[]{:S(2)}, u32[]{:S(2)}) %all-to-all-start) | async-done | bytes 393248 | tf_op jit(solution)/shard_map/all_to_all | solution.py:360
  28.7 1.0 %shard_map.68 = bf16[32,1,3,16,128]{4,3,2,1,0:T(8,128)(2,1)} custom-call(bf16[32,1,3,16,128]{4,3,2,1,0:T(8,128)(2,1)S(1)} %bitcast.2), custom_call_target="tpu_custom_call" | custom-call | flops 1048576 | bytes 1572864 | tf_op jit(solution)/shard_map/pallas_call | solution.py:361
  29.6 4.8 %all-to-all-start.1 = ((bf16[32,3,16,128]{3,2,1,0:T(8,128)(2,1)}), bf16[32,3,16,128]{3,2,1,0:T(8,128)(2,1)S(1)}, u32[]{:S(2)}, u32[]{:S(2)}) async-start(bf16[32,3,16,128]{3,2,1,0:T(8,128)(2,1)} %bitcast.1), calls=%async_computation.1 | async-start | bytes 786432 | tf_op jit(solution)/shard_map/all_to_all | solution.py:369
  34.4 0.0 collective-permute-done
  34.4 0.0 collective-permute-done.1
  34.4 0.2 pad_maximum_fusion.edge_ref
  34.6 0.0 copy-done.1
  34.6 0.0 copy-done.3
  34.6 0.0 copy-done.2
  34.6 0.0 copy-start
  34.6 1.0 %copy-done = bf16[4,16,4096]{2,1,0:T(8,128)(2,1)S(1)} copy-done((bf16[4,16,4096]{2,1,0:T(8,128)(2,1)S(1)}, bf16[4,16,4096]{2,1,0:T(8,128)(2,1)}, u32[]{:S(2)}) %copy-start) | copy-done | bytes 524312
  35.7 3.9 %shard_map.69.local_ref = f32[4,3,32,16,128]{4,3,2,1,0:T(8,128)S(1)} custom-call(f32[4]{0:T(128)S(1)} %copy-done.2, f32[4]{0:T(128)S(1)} %copy-done.3, f32[4]{0:T(128)S(1)} %copy-done.1, bf16[4,16,4096]{2,1,0:T(8,128)(2,1)S(1)} %copy-done, bf16[4,8,4096]{2,1,0:T(8,128)(2,1)S(1)} %pad_maximum_fusion.edge_ref), custom_call_target="tpu_custom_call" | custom-call | flops 15728640 | bytes 5242880 | tf_op jit(solution)/shard_map/pallas_call | solution.py:372
  39.6 9.3 %all-to-all-done.1.pre_ref = bf16[32,3,16,128]{3,2,1,0:T(8,128)(2,1)S(1)} async-done(((bf16[32,3,16,128]{3,2,1,0:T(8,128)(2,1)}), bf16[32,3,16,128]{3,2,1,0:T(8,128)(2,1)S(1)}, u32[]{:S(2)}, u32[]{:S(2)}) %all-to-all-start.1) | async-done | bytes 393248 | tf_op jit(solution)/shard_map/all_to_all | solution.py:369
  48.9 0.1 fusion.1
  49.0 0.3 collective-permute-start.2
  49.3 0.2 collective-permute-start.3
  49.5 2.9 %shard_map.70.own_ref = f32[4,3,32,16,128]{4,3,2,1,0:T(8,128)S(1)} custom-call(f32[4]{0:T(128)S(1)} %copy-done.1, bf16[32,3,16,128]{3,2,1,0:T(8,128)(2,1)S(1)} %all-to-all-done.1.pre_ref, f32[4,3,32,16,128]{4,3,2,1,0:T(8,128)S(1)} %shard_map.69.local_ref), custom_call_target="tpu_custom_call" | custom-call | flops 7864320 | bytes 5242880 | tf_op jit(solution)/shard_map/pallas_call | solution.py:385
  52.4 0.0 collective-permute-done.2
  52.4 1.6 %collective-permute-done.3 = bf16[32,3,2,128]{3,2,1,0:T(2,128)(2,1)S(1)} collective-permute-done((bf16[32,3,2,128]{3,2,1,0:T(2,128)(2,1)S(1)}, bf16[32,3,2,128]{3,2,1,0:T(2,128)(2,1)S(1)}, u32[]{:S(2)}, u32[]{:S(2)}) %collective-permute-start.3) | collective-permute-done | bytes 49184 | tf_op jit(solution)/shard_map/ppermute | solution.py:383
  54.0 0.1 pad_maximum_fusion.1.edge_ref
  54.1 2.5 %shard_map.71 = (bf16[4,16,4096]{2,1,0:T(8,128)(2,1)}, bf16[4,16,4096]{2,1,0:T(8,128)(2,1)}, bf16[4,16,4096]{2,1,0:T(8,128)(2,1)}) custom-call(f32[4]{0:T(128)S(1)} %copy-done.1, bf16[32,3,8,128]{3,2,1,0:T(8,128)(2,1)S(1)} %pad_maximum_fusion.1.edge_ref, f32[4,3,32,16,128]{4,3,2,1,0:T(8,128)S(1)} %shard_map.70.own_ref), custom_call_target="tpu_custom_call" | custom-call | flops 10485760 | bytes 5242880 | tf_op jit(solution)/shard_map/pallas_call | solution.py:397
  (1 shorter events, 0.0 us)
Async XLA Ops:
  0.6 34.0 %copy-start.1 = (f32[4]{0:T(128)S(1)}, f32[4]{0:T(128)}, u32[]{:S(2)}) copy-start(f32[4]{0:T(128)} %source_ref.5) | copy-start | bytes 52
  0.6 34.0 %copy-start.3 = (f32[4]{0:T(128)S(1)}, f32[4]{0:T(128)}, u32[]{:S(2)}) copy-start(f32[4]{0:T(128)} %dist_ref.1) | copy-start | bytes 52
  0.7 34.0 %copy-start.2 = (f32[4]{0:T(128)S(1)}, f32[4]{0:T(128)}, u32[]{:S(2)}) copy-start(f32[4]{0:T(128)} %weight_ref.1) | copy-start | bytes 52
  2.6 26.1 %all-to-all-start = ((bf16[32,3,16,128]{3,2,1,0:T(8,128)(2,1)}), bf16[32,3,16,128]{3,2,1,0:T(8,128)(2,1)S(1)}, u32[]{:S(2)}, u32[]{:S(2)}) async-start(bf16[32,3,16,128]{3,2,1,0:T(8,128)(2,1)} %shard_map.67), calls=%async_computation | async-start | bytes 786432 | tf_op jit(solution)/shard_map/all_to_all | solution.py:360
  14.9 19.5 %collective-permute-start = (bf16[4,2,4096]{2,1,0:T(2,128)(2,1)S(1)}, bf16[4,2,4096]{2,1,0:T(2,128)(2,1)S(1)}, u32[]{:S(2)}, u32[]{:S(2)}) collective-permute-start(bf16[4,2,4096]{2,1,0:T(2,128)(2,1)S(1)} %get-tuple-element.7), channel_id=1, source_target_pairs={{1,0},{2,1},{3,2},{4,3},{5,4},{6,5},{7,6},{0,7},{9,8},{10,9},{11,1... | collective-permute-start | bytes 196616 | tf_op jit(solution)/shard_map/ppermute | solution.py:340
  16.8 17.6 %collective-permute-start.1 = (bf16[4,2,4096]{2,1,0:T(2,128)(2,1)S(1)}, bf16[4,2,4096]{2,1,0:T(2,128)(2,1)S(1)}, u32[]{:S(2)}, u32[]{:S(2)}) collective-permute-start(bf16[4,2,4096]{2,1,0:T(2,128)(2,1)S(1)} %get-tuple-element.8), channel_id=1, source_target_pairs={{0,1},{1,2},{2,3},{3,4},{4,5},{5,6},{6,7},{7,0},{8,9},{9,10},{10,1... | collective-permute-start | bytes 196616 | tf_op jit(solution)/shard_map/ppermute | solution.py:339
  29.6 19.3 %all-to-all-start.1 = ((bf16[32,3,16,128]{3,2,1,0:T(8,128)(2,1)}), bf16[32,3,16,128]{3,2,1,0:T(8,128)(2,1)S(1)}, u32[]{:S(2)}, u32[]{:S(2)}) async-start(bf16[32,3,16,128]{3,2,1,0:T(8,128)(2,1)} %bitcast.1), calls=%async_computation.1 | async-start | bytes 786432 | tf_op jit(solution)/shard_map/all_to_all | solution.py:369
  34.6 1.0 %copy-start = (bf16[4,16,4096]{2,1,0:T(8,128)(2,1)S(1)}, bf16[4,16,4096]{2,1,0:T(8,128)(2,1)}, u32[]{:S(2)}) copy-start(bf16[4,16,4096]{2,1,0:T(8,128)(2,1)} %pot_ref.1) | copy-start | bytes 1572868
  49.0 3.4 %collective-permute-start.2 = (bf16[32,3,2,128]{3,2,1,0:T(2,128)(2,1)S(1)}, bf16[32,3,2,128]{3,2,1,0:T(2,128)(2,1)S(1)}, u32[]{:S(2)}, u32[]{:S(2)}) collective-permute-start(bf16[32,3,2,128]{3,2,1,0:T(2,128)(2,1)S(1)} %get-tuple-element.9), channel_id=1, source_target_pairs={{1,0},{2,1},{3,2},{4,3},{5,4},{6,5},{7,6},{0,7},{9,8},{10,9},{11,1... | collective-permute-start | bytes 147464 | tf_op jit(solution)/shard_map/ppermute | solution.py:384
  49.3 4.7 %collective-permute-start.3 = (bf16[32,3,2,128]{3,2,1,0:T(2,128)(2,1)S(1)}, bf16[32,3,2,128]{3,2,1,0:T(2,128)(2,1)S(1)}, u32[]{:S(2)}, u32[]{:S(2)}) collective-permute-start(bf16[32,3,2,128]{3,2,1,0:T(2,128)(2,1)S(1)} %get-tuple-element.10), channel_id=1, source_target_pairs={{0,1},{1,2},{2,3},{3,4},{4,5},{5,6},{6,7},{7,0},{8,9},{9,10},{10,1... | collective-permute-start | bytes 147464 | tf_op jit(solution)/shard_map/ppermute | solution.py:383

commit v4 on v3

--- a/solution.py
+++ b/solution.py
@@ -50,7 +50,8 @@
     r2 = pltpu.roll(jnp.where(lane >= LANES - 2, prev, here), 2, 1)
     l1 = pltpu.roll(jnp.where(lane == 0, nxt, here), LANES - 1, 1)
     l2 = pltpu.roll(jnp.where(lane < 2, nxt, here), LANES - 2, 1)
-    return 8.0 * (l1 - r1) - (l2 - r2), 16.0 * (l1 + r1) - (l2 + r2)
+    first = 8.0 * (l1 - r1) - (l2 - r2)
+    return first, (16.0 * SCALE) * (l1 + r1) - SCALE * (l2 + r2)
 
 
 def shifts_y(tiles, edge, row):
@@ -69,11 +70,11 @@
 
 
 def second_y(d1, d2, u1, u2):
-    return 16.0 * (u1 + d1) - (u2 + d2)
+    return (16.0 * SCALE) * (u1 + d1) - SCALE * (u2 + d2)
 
 
 def first_y(d1, d2, u1, u2):
-    return 8.0 * (u1 - d1) - (u2 - d2)
+    return (8.0 * SCALE_CROSS) * (u1 - d1) - SCALE_CROSS * (u2 - d2)
 
 
 def spread(ref, shape):
@@ -150,12 +151,14 @@
         copy.wait()
 
 
-def earlier_kernel(in_ref, out_ref):
+def earlier_kernel(in_ref, out_hbm, out_ref, sems):
     count, per = in_ref.shape[0], in_ref.shape[1]
     shape = in_ref.shape[3:]
     row = lax.broadcasted_iota(jnp.int32, shape, 0)
     lane = lax.broadcasted_iota(jnp.int32, shape, 1)
     taken = (row == 0) & (lane < 2)
+    part = -(-count // STEPS)
+    copies = []
     for q in range(per):
         run_near = jnp.zeros(shape, F32)
         run_far = run_near
@@ -171,6 +174,12 @@
                 total = in_ref[i, q, 0].astype(F32) + jnp.where(taken, 0.0, low)
                 run_near = run_near + total
                 run_far = run_far + (dist_mid * total + in_ref[i, q, 2].astype(F32))
+            if q == per - 1 and ((i + 1) % part == 0 or i == count - 1):
+                at = pl.ds(i // part * part, i % part + 1)
+                copies.append(pltpu.make_async_copy(out_ref.at[at], out_hbm.at[at], sems.at[len(copies)]))
+                copies[-1].start()
+    for copy in copies:
+        copy.wait()
 
 
 def local_kernel(weight_ref, dist_ref, source_ref, pot_ref, edge_ref, out_ref, lens):
@@ -213,7 +222,7 @@
             for k in range(height // SUB):
                 at = slice(k * SUB, (k + 1) * SUB)
                 sy = second_y(*ys[k])
-                out_ref[s, 0, c, at] = (seconds[k + 1] + sy) - 60.0 * here[k + 1]
+                out_ref[s, 0, c, at] = (seconds[k + 1] + sy) - (60.0 * SCALE) * here[k + 1]
                 out_ref[s, 1, c, at] = seconds[k + 1] - sy
                 out_ref[s, 2, c, at] = first_y(*cs[k])
         return carry
@@ -227,11 +236,13 @@
     return ref[c, 0, at : at + size].astype(F32) + ref[c, 1, at : at + size].astype(F32)
 
 
-def own_kernel(source_ref, pre_ref, local_ref, out_ref, field):
+def own_kernel(source_ref, pre_ref, local_ref, out_ref, slope_ref, field):
     chunks, height = pre_ref.shape[0], pre_ref.shape[2]
     planes = local_ref.shape[0]
     inv, inv_mid = inverses(source_ref, (SUB, LANES))
     slope = [inv_mid - v for v in inv]
+    for s in range(planes):
+        slope_ref[s] = slope[s]
 
     def build(c, carry):
         for f in range(2):
@@ -258,29 +269,29 @@
             cs = shifts_y(firsts, zero, row)
             for k in range(height // SUB):
                 sy = second_y(*ys[k])
-                parts.append(((seconds[k] + sy) - 60.0 * here[k], seconds[k] - sy, first_y(*cs[k])))
+                parts.append(((seconds[k] + sy) - (60.0 * SCALE) * here[k], seconds[k] - sy, first_y(*cs[k])))
         for k in range(height // SUB):
             at = slice(k * SUB, (k + 1) * SUB)
-            for n, scale in enumerate((SCALE, SCALE, SCALE_CROSS)):
+            for n in range(3):
                 lens, far = parts[k][n], parts[height // SUB + k][n]
                 for s in range(planes):
-                    out_ref[s, n, c, at] = (local_ref[s, n, c, at] + lens + slope[s] * far) * scale
-        return carry
-
-    lax.fori_loop(0, chunks, sten, 0, unroll=2)
-
-
-def join_kernel(source_ref, edge_ref, own_ref, conv_hbm, one_hbm, two_hbm, conv_ref, one_ref, two_ref, field, sems):
+                    out_ref[s, n, c, at] = (local_ref[s, n, c, at] + lens) + slope[s] * far
+        return carry
+
+    lax.fori_loop(0, chunks, sten, 0, unroll=4)
+
+
+def join_kernel(slope_ref, before_ref, after_ref, own_ref, conv_hbm, one_hbm, two_hbm, conv_ref, one_ref, two_ref, field, sems):
     planes, chunks, height = own_ref.shape[0], own_ref.shape[2], own_ref.shape[3]
     per = chunks // STEPS
-    inv, inv_mid = inverses(source_ref, (SUB, LANES))
-    slope = [inv_mid - v for v in inv]
+    slope = [slope_ref[s] for s in range(planes)]
     row, lane = iotas()
     tiles = height // SUB
 
     def build(c, carry):
         for f in range(2):
-            field[f, c] = field_of(edge_ref, c, f, 0, SUB)
+            field[f, c, :2] = field_of(after_ref, c, f, 0, 2)
+            field[f, c, SUB - 2 :] = field_of(before_ref, c, f, 0, 2)
         return carry
 
     lax.fori_loop(0, chunks, build, 0, unroll=8)
@@ -362,7 +373,11 @@
         earlier_kernel,
         out_shape=jax.ShapeDtypeStruct((count, chunks // count) + piece, BF16),
         in_specs=[VMEM],
-        out_specs=VMEM,
+        out_specs=ANY,
+        scratch_shapes=[
+            pltpu.VMEM((count, chunks // count) + piece, BF16),
+            pltpu.SemaphoreType.DMA((STEPS,)),
+        ],
         compiler_params=params(),
         cost_estimate=cost(4 * size, 6 * size),
     )(received.reshape((count, chunks // count) + piece))
@@ -382,22 +397,20 @@
 
     pre_before = lax.ppermute(prefix[:, :, height - 2 :], "sky", forward)
     pre_after = lax.ppermute(prefix[:, :, :2], "sky", backward)
-    own = pl.pallas_call(
+    own, slope = pl.pallas_call(
         own_kernel,
-        out_shape=grids,
+        out_shape=[grids, f32(shells, SUB, LANES)],
         in_specs=[SMEM] + [VMEM] * 2,
-        out_specs=VMEM,
+        out_specs=[VMEM] * 2,
         scratch_shapes=[pltpu.VMEM((2, chunks, height, LANES), F32)],
         compiler_params=params(),
         cost_estimate=cost(30 * size, 20 * size),
     )(source_dist, prefix, local)
-    pre_edge = jnp.concatenate([pre_after, jnp.zeros((chunks, 3, SUB - 4, LANES), BF16), pre_before], 2)
-
     return tuple(
         pl.pallas_call(
             join_kernel,
             out_shape=[jax.ShapeDtypeStruct(potentials.shape, BF16)] * 3,
-            in_specs=[SMEM] + [VMEM] * 2,
+            in_specs=[VMEM] * 4,
             out_specs=[ANY] * 3,
             scratch_shapes=[
                 *[pltpu.VMEM(potentials.shape, BF16)] * 3,
@@ -406,7 +419,7 @@
             ],
             compiler_params=params(),
             cost_estimate=cost(40 * size, 20 * size),
-        )(source_dist, pre_edge, own)
+        )(slope, pre_before, pre_after, own)
     )
 
 

time: 57.2 us -> 56.3 us (0.984)
  Pallas kernels: 12.2 us -> 10.9 us
  waiting for transfers between devices: 22.6 us -> 23.4 us
    pallas_call x1, Pallas kernels: 2.91 us -> 2.16 us  [on_device(): pl.pallas_call(own_kernel, out_shape=[grids, f32(shells, SUB, LANES)], in...]
    ppermute x1, waiting for transfers between devices: 1.58 us -> 2.33 us  [on_device(): pre_before = lax.ppermute(prefix[:, :, height - 2:], 'sky', forward)]
  transfers between devices with their start and end apart: 6 -> 6, of which waited for: 3 -> 3; matrix products, arithmetic and copies ran while one was open for 2% -> 2% of each run, Pallas kernels for 14% -> 12%
where the time goes in v4:
time: 56.3 us; the launch traced here: 56 us
  waiting for transfers between devices  23.4 us (42%)
  starting transfers between devices  18.4 us (33%)
  Pallas kernels  10.9 us (19%)
  local copies, waits for them, and re-layouts  2.35 us (4%)
  between operations  0.77 us (1%)
    all_to_all x1, waiting for transfers between devices, on_device(): lax.all_to_all(totals, 'los', split_axis=0, concat_axis=0, tiled=True)  11.7 us
    all_to_all x1, starting transfers between devices, on_device(): lax.all_to_all(totals, 'los', split_axis=0, concat_axis=0, tiled=True)  11.2 us
    all_to_all x1, waiting for transfers between devices, on_device(): lax.all_to_all(earlier.reshape((chunks,) + piece), 'los', split_axis=0, c...  9.29 us
    all_to_all x1, starting transfers between devices, on_device(): lax.all_to_all(earlier.reshape((chunks,) + piece), 'los', split_axis=0, c...  4.79 us
    pallas_call x1, Pallas kernels, on_device(): pl.pallas_call(local_kernel, out_shape=grids, in_specs=[SMEM, SMEM, SMEM,...  3.91 us
    ppermute x1, waiting for transfers between devices, on_device(): pre_before = lax.ppermute(prefix[:, :, height - 2:], 'sky', forward)  2.33 us
    pallas_call x1, Pallas kernels, on_device(): pl.pallas_call(own_kernel, out_shape=[grids, f32(shells, SUB, LANES)], in...  2.16 us
    pallas_call x1, Pallas kernels, on_device(): pl.pallas_call(join_kernel, out_shape=[jax.ShapeDtypeStruct(potentials.sh...  2 us
  transfers between devices with their start and end apart: 6, of which 3 were waited for; matrix products, arithmetic and copies ran while one was open for 2% of the time, Pallas kernels for 12%

profile of v4, /device:TPU:32, one launch (start us, length us, event | category | flops | bytes accessed | tf_op | source)
XLA Modules:
  0.0 56.0 jit_solution(1904653851144455479)
XLA Ops:
  0.6 0.0 copy-start.1
  0.6 0.0 copy-start.3
  0.7 0.0 copy-start.2
  0.7 1.9 %shard_map.67 = bf16[32,3,16,128]{3,2,1,0:T(8,128)(2,1)} custom-call(f32[4]{0:T(128)} %weight_ref.1, f32[4]{0:T(128)} %dist_ref.1, f32[4]{0:T(128)} %source_ref.3, bf16[4,16,4096]{2,1,0:T(8,128)(2,1)} %pot_ref.1), custom_call_target="tpu_custom_call" | custom-call | flops 1048576 | bytes 1572864 | tf_op jit(solution)/shard_map/pallas_call | solution.py:355
  2.6 11.2 %all-to-all-start = ((bf16[32,3,16,128]{3,2,1,0:T(8,128)(2,1)}), bf16[32,3,16,128]{3,2,1,0:T(8,128)(2,1)S(1)}, u32[]{:S(2)}, u32[]{:S(2)}) async-start(bf16[32,3,16,128]{3,2,1,0:T(8,128)(2,1)} %shard_map.67), calls=%async_computation | async-start | bytes 786432 | tf_op jit(solution)/shard_map/all_to_all | solution.py:371
  13.8 1.1 %fusion = (bf16[4,2,4096]{2,1,0:T(2,128)(2,1)S(1)}, bf16[4,2,4096]{2,1,0:T(2,128)(2,1)S(1)}) fusion(bf16[4,16,4096]{2,1,0:T(8,128)(2,1)} %pot_ref.1), kind=kLoop, calls=%fused_computation.1 | loop fusion | bytes 262144 | tf_op jit(solution)/shard_map/slice | solution.py:351
  14.9 1.9 %collective-permute-start = (bf16[4,2,4096]{2,1,0:T(2,128)(2,1)S(1)}, bf16[4,2,4096]{2,1,0:T(2,128)(2,1)S(1)}, u32[]{:S(2)}, u32[]{:S(2)}) collective-permute-start(bf16[4,2,4096]{2,1,0:T(2,128)(2,1)S(1)} %get-tuple-element.11), channel_id=1, source_target_pairs={{1,0},{2,1},{3,2},{4,3},{5,4},{6,5},{7,6},{0,7},{9,8},{10,9},{11,1... | collective-permute-start | bytes 196616 | tf_op jit(solution)/shard_map/ppermute | solution.py:351
  16.8 0.0 collective-permute-start.1
  16.8 0.1 pad.1.clone
  16.9 11.7 %all-to-all-done = bf16[32,3,16,128]{3,2,1,0:T(8,128)(2,1)S(1)} async-done(((bf16[32,3,16,128]{3,2,1,0:T(8,128)(2,1)}), bf16[32,3,16,128]{3,2,1,0:T(8,128)(2,1)S(1)}, u32[]{:S(2)}, u32[]{:S(2)}) %all-to-all-start) | async-done | bytes 393248 | tf_op jit(solution)/shard_map/all_to_all | solution.py:371
  28.7 0.9 %shard_map.68 = bf16[32,1,3,16,128]{4,3,2,1,0:T(8,128)(2,1)} custom-call(bf16[32,1,3,16,128]{4,3,2,1,0:T(8,128)(2,1)S(1)} %bitcast.2), custom_call_target="tpu_custom_call" | custom-call | flops 1048576 | bytes 1572864 | tf_op jit(solution)/shard_map/pallas_call | solution.py:372
  29.6 4.8 %all-to-all-start.1 = ((bf16[32,3,16,128]{3,2,1,0:T(8,128)(2,1)}), bf16[32,3,16,128]{3,2,1,0:T(8,128)(2,1)S(1)}, u32[]{:S(2)}, u32[]{:S(2)}) async-start(bf16[32,3,16,128]{3,2,1,0:T(8,128)(2,1)} %bitcast.1), calls=%async_computation.1 | async-start | bytes 786432 | tf_op jit(solution)/shard_map/all_to_all | solution.py:384
  34.4 0.0 collective-permute-done
  34.4 0.0 collective-permute-done.1
  34.4 0.2 pad_maximum_fusion.edge_ref
  34.6 0.0 copy-done.1
  34.6 0.0 copy-done.3
  34.6 0.0 copy-done.2
  34.6 0.0 copy-start
  34.6 1.0 %copy-done = bf16[4,16,4096]{2,1,0:T(8,128)(2,1)S(1)} copy-done((bf16[4,16,4096]{2,1,0:T(8,128)(2,1)S(1)}, bf16[4,16,4096]{2,1,0:T(8,128)(2,1)}, u32[]{:S(2)}) %copy-start) | copy-done | bytes 524312
  35.6 3.9 %shard_map.69.local_ref = f32[4,3,32,16,128]{4,3,2,1,0:T(8,128)S(1)} custom-call(f32[4]{0:T(128)S(1)} %copy-done.2, f32[4]{0:T(128)S(1)} %copy-done.3, f32[4]{0:T(128)S(1)} %copy-done.1, bf16[4,16,4096]{2,1,0:T(8,128)(2,1)S(1)} %copy-done, bf16[4,8,4096]{2,1,0:T(8,128)(2,1)S(1)} %pad_maximum_fusion.edge_ref), custom_call_target="tpu_custom_call" | custom-call | flops 15728640 | bytes 5242880 | tf_op jit(solution)/shard_map/pallas_call | solution.py:387
  39.6 9.3 %all-to-all-done.1.pre_ref = bf16[32,3,16,128]{3,2,1,0:T(8,128)(2,1)S(1)} async-done(((bf16[32,3,16,128]{3,2,1,0:T(8,128)(2,1)}), bf16[32,3,16,128]{3,2,1,0:T(8,128)(2,1)S(1)}, u32[]{:S(2)}, u32[]{:S(2)}) %all-to-all-start.1) | async-done | bytes 393248 | tf_op jit(solution)/shard_map/all_to_all | solution.py:384
  48.8 0.1 fusion.1
  48.9 0.3 collective-permute-start.3
  49.2 0.2 collective-permute-start.2
  49.5 2.2 %shard_map.70 = (f32[4,3,32,16,128]{4,3,2,1,0:T(8,128)S(1)}, f32[4,8,128]{2,1,0:T(8,128)S(1)}) custom-call(f32[4]{0:T(128)S(1)} %copy-done.1, bf16[32,3,16,128]{3,2,1,0:T(8,128)(2,1)S(1)} %all-to-all-done.1.pre_ref, f32[4,3,32,16,128]{4,3,2,1,0:T(8,128)S(1)} %shard_map.69.local_ref), custom_call_target="tpu_custom_call" | custom-call | flops 7864320 | bytes 5242880 | tf_op jit(solution)/shard_map/pallas_call | solution.py:400
  51.6 0.0 collective-permute-done.3.after_ref
  51.6 2.3 %collective-permute-done.2.before_ref = bf16[32,3,2,128]{3,2,1,0:T(2,128)(2,1)S(1)} collective-permute-done((bf16[32,3,2,128]{3,2,1,0:T(2,128)(2,1)S(1)}, bf16[32,3,2,128]{3,2,1,0:T(2,128)(2,1)S(1)}, u32[]{:S(2)}, u32[]{:S(2)}) %collective-permute-start.2) | collective-permute-done | bytes 49184 | tf_op jit(solution)/shard_map/ppermute | solution.py:398
  54.0 2.0 %shard_map.71 = (bf16[4,16,4096]{2,1,0:T(8,128)(2,1)}, bf16[4,16,4096]{2,1,0:T(8,128)(2,1)}, bf16[4,16,4096]{2,1,0:T(8,128)(2,1)}) custom-call(f32[4,8,128]{2,1,0:T(8,128)S(1)} %get-tuple-element.9.slope_ref, bf16[32,3,2,128]{3,2,1,0:T(2,128)(2,1)S(1)} %collective-permute-done.2.before_ref, bf16[32,3,2,128]{3,2,1,0:T(2,128)(2,1)S(1)} %collective-permute-done.3.after_ref, ...), custom_call_target="tpu_custom_call" | custom-call | flops 10485760 | bytes 5242880 | tf_op jit(solution)/shard_map/pallas_call | solution.py:410
  (1 shorter events, 0.0 us)
Async XLA Ops:
  0.6 33.9 %copy-start.1 = (f32[4]{0:T(128)S(1)}, f32[4]{0:T(128)}, u32[]{:S(2)}) copy-start(f32[4]{0:T(128)} %source_ref.3) | copy-start | bytes 52
  0.6 33.9 %copy-start.3 = (f32[4]{0:T(128)S(1)}, f32[4]{0:T(128)}, u32[]{:S(2)}) copy-start(f32[4]{0:T(128)} %dist_ref.1) | copy-start | bytes 52
  0.7 33.9 %copy-start.2 = (f32[4]{0:T(128)S(1)}, f32[4]{0:T(128)}, u32[]{:S(2)}) copy-start(f32[4]{0:T(128)} %weight_ref.1) | copy-start | bytes 52
  2.6 26.1 %all-to-all-start = ((bf16[32,3,16,128]{3,2,1,0:T(8,128)(2,1)}), bf16[32,3,16,128]{3,2,1,0:T(8,128)(2,1)S(1)}, u32[]{:S(2)}, u32[]{:S(2)}) async-start(bf16[32,3,16,128]{3,2,1,0:T(8,128)(2,1)} %shard_map.67), calls=%async_computation | async-start | bytes 786432 | tf_op jit(solution)/shard_map/all_to_all | solution.py:371
  14.9 19.5 %collective-permute-start = (bf16[4,2,4096]{2,1,0:T(2,128)(2,1)S(1)}, bf16[4,2,4096]{2,1,0:T(2,128)(2,1)S(1)}, u32[]{:S(2)}, u32[]{:S(2)}) collective-permute-start(bf16[4,2,4096]{2,1,0:T(2,128)(2,1)S(1)} %get-tuple-element.11), channel_id=1, source_target_pairs={{1,0},{2,1},{3,2},{4,3},{5,4},{6,5},{7,6},{0,7},{9,8},{10,9},{11,1... | collective-permute-start | bytes 196616 | tf_op jit(solution)/shard_map/ppermute | solution.py:351
  16.8 17.6 %collective-permute-start.1 = (bf16[4,2,4096]{2,1,0:T(2,128)(2,1)S(1)}, bf16[4,2,4096]{2,1,0:T(2,128)(2,1)S(1)}, u32[]{:S(2)}, u32[]{:S(2)}) collective-permute-start(bf16[4,2,4096]{2,1,0:T(2,128)(2,1)S(1)} %get-tuple-element.12), channel_id=1, source_target_pairs={{0,1},{1,2},{2,3},{3,4},{4,5},{5,6},{6,7},{7,0},{8,9},{9,10},{10,1... | collective-permute-start | bytes 196616 | tf_op jit(solution)/shard_map/ppermute | solution.py:350
  29.6 19.3 %all-to-all-start.1 = ((bf16[32,3,16,128]{3,2,1,0:T(8,128)(2,1)}), bf16[32,3,16,128]{3,2,1,0:T(8,128)(2,1)S(1)}, u32[]{:S(2)}, u32[]{:S(2)}) async-start(bf16[32,3,16,128]{3,2,1,0:T(8,128)(2,1)} %bitcast.1), calls=%async_computation.1 | async-start | bytes 786432 | tf_op jit(solution)/shard_map/all_to_all | solution.py:384
  34.6 1.0 %copy-start = (bf16[4,16,4096]{2,1,0:T(8,128)(2,1)S(1)}, bf16[4,16,4096]{2,1,0:T(8,128)(2,1)}, u32[]{:S(2)}) copy-start(bf16[4,16,4096]{2,1,0:T(8,128)(2,1)} %pot_ref.1) | copy-start | bytes 1572868
  48.9 2.7 %collective-permute-start.3 = (bf16[32,3,2,128]{3,2,1,0:T(2,128)(2,1)S(1)}, bf16[32,3,2,128]{3,2,1,0:T(2,128)(2,1)S(1)}, u32[]{:S(2)}, u32[]{:S(2)}) collective-permute-start(bf16[32,3,2,128]{3,2,1,0:T(2,128)(2,1)S(1)} %get-tuple-element.13), channel_id=1, source_target_pairs={{1,0},{2,1},{3,2},{4,3},{5,4},{6,5},{7,6},{0,7},{9,8},{10,9},{11,1... | collective-permute-start | bytes 147464 | tf_op jit(solution)/shard_map/ppermute | solution.py:399
  49.2 4.7 %collective-permute-start.2 = (bf16[32,3,2,128]{3,2,1,0:T(2,128)(2,1)S(1)}, bf16[32,3,2,128]{3,2,1,0:T(2,128)(2,1)S(1)}, u32[]{:S(2)}, u32[]{:S(2)}) collective-permute-start(bf16[32,3,2,128]{3,2,1,0:T(2,128)(2,1)S(1)} %get-tuple-element.14), channel_id=1, source_target_pairs={{0,1},{1,2},{2,3},{3,4},{4,5},{5,6},{6,7},{7,0},{8,9},{9,10},{10,1... | collective-permute-start | bytes 147464 | tf_op jit(solution)/shard_map/ppermute | solution.py:398

commit v5 on v4

--- a/solution.py
+++ b/solution.py
@@ -9,7 +9,7 @@
 
 LANES = 128
 SUB = 8
-STEPS = 4
+STEPS = 8
 SCALE = 1.0 / 24.0
 SCALE_CROSS = 1.0 / 144.0
 VMEM = pl.BlockSpec(memory_space=pltpu.VMEM)

time: 56.3 us -> 56.1 us (level)
  transfers between devices with their start and end apart: 6 -> 6, of which waited for: 3 -> 3; matrix products, arithmetic and copies ran while one was open for 2% -> 2% of each run, Pallas kernels for 12% -> 13%
where the time goes in v5:
time: 56.1 us; the launch traced here: 55.7 us
  waiting for transfers between devices  23.4 us (42%)
  starting transfers between devices  18.4 us (33%)
  Pallas kernels  10.6 us (19%)
  local copies, waits for them, and re-layouts  2.35 us (4%)
  between operations  0.77 us (1%)
    all_to_all x1, waiting for transfers between devices, on_device(): lax.all_to_all(totals, 'los', split_axis=0, concat_axis=0, tiled=True)  11.7 us
    all_to_all x1, starting transfers between devices, on_device(): lax.all_to_all(totals, 'los', split_axis=0, concat_axis=0, tiled=True)  11.2 us
    all_to_all x1, waiting for transfers between devices, on_device(): lax.all_to_all(earlier.reshape((chunks,) + piece), 'los', split_axis=0, c...  9.29 us
    all_to_all x1, starting transfers between devices, on_device(): lax.all_to_all(earlier.reshape((chunks,) + piece), 'los', split_axis=0, c...  4.79 us
    pallas_call x1, Pallas kernels, on_device(): pl.pallas_call(local_kernel, out_shape=grids, in_specs=[SMEM, SMEM, SMEM,...  3.91 us
    ppermute x1, waiting for transfers between devices, on_device(): pre_before = lax.ppermute(prefix[:, :, height - 2:], 'sky', forward)  2.33 us
    pallas_call x1, Pallas kernels, on_device(): pl.pallas_call(own_kernel, out_shape=[grids, f32(shells, SUB, LANES)], in...  2.16 us
    ppermute x1, starting transfers between devices, on_device(): pot_after = lax.ppermute(potentials[:, :2], 'sky', backward)  1.91 us
  transfers between devices with their start and end apart: 6, of which 3 were waited for; matrix products, arithmetic and copies ran while one was open for 2% of the time, Pallas kernels for 13%

profile of v5, /device:TPU:32, one launch (start us, length us, event | category | flops | bytes accessed | tf_op | source)
XLA Modules:
  0.0 55.7 jit_solution(2908826848642527828)
XLA Ops:
  0.6 0.0 copy-start.1
  0.6 0.0 copy-start.3
  0.7 0.0 copy-start.2
  0.7 1.9 %shard_map.67 = bf16[32,3,16,128]{3,2,1,0:T(8,128)(2,1)} custom-call(f32[4]{0:T(128)} %weight_ref.1, f32[4]{0:T(128)} %dist_ref.1, f32[4]{0:T(128)} %source_ref.3, bf16[4,16,4096]{2,1,0:T(8,128)(2,1)} %pot_ref.1), custom_call_target="tpu_custom_call" | custom-call | flops 1048576 | bytes 1572864 | tf_op jit(solution)/shard_map/pallas_call | solution.py:355
  2.6 11.2 %all-to-all-start = ((bf16[32,3,16,128]{3,2,1,0:T(8,128)(2,1)}), bf16[32,3,16,128]{3,2,1,0:T(8,128)(2,1)S(1)}, u32[]{:S(2)}, u32[]{:S(2)}) async-start(bf16[32,3,16,128]{3,2,1,0:T(8,128)(2,1)} %shard_map.67), calls=%async_computation | async-start | bytes 786432 | tf_op jit(solution)/shard_map/all_to_all | solution.py:371
  13.8 1.1 %fusion = (bf16[4,2,4096]{2,1,0:T(2,128)(2,1)S(1)}, bf16[4,2,4096]{2,1,0:T(2,128)(2,1)S(1)}) fusion(bf16[4,16,4096]{2,1,0:T(8,128)(2,1)} %pot_ref.1), kind=kLoop, calls=%fused_computation.1 | loop fusion | bytes 262144 | tf_op jit(solution)/shard_map/slice | solution.py:351
  14.9 1.9 %collective-permute-start = (bf16[4,2,4096]{2,1,0:T(2,128)(2,1)S(1)}, bf16[4,2,4096]{2,1,0:T(2,128)(2,1)S(1)}, u32[]{:S(2)}, u32[]{:S(2)}) collective-permute-start(bf16[4,2,4096]{2,1,0:T(2,128)(2,1)S(1)} %get-tuple-element.11), channel_id=1, source_target_pairs={{1,0},{2,1},{3,2},{4,3},{5,4},{6,5},{7,6},{0,7},{9,8},{10,9},{11,1... | collective-permute-start | bytes 196616 | tf_op jit(solution)/shard_map/ppermute | solution.py:351
  16.8 0.0 collective-permute-start.1
  16.8 0.1 pad.1.clone
  16.9 11.7 %all-to-all-done = bf16[32,3,16,128]{3,2,1,0:T(8,128)(2,1)S(1)} async-done(((bf16[32,3,16,128]{3,2,1,0:T(8,128)(2,1)}), bf16[32,3,16,128]{3,2,1,0:T(8,128)(2,1)S(1)}, u32[]{:S(2)}, u32[]{:S(2)}) %all-to-all-start) | async-done | bytes 393248 | tf_op jit(solution)/shard_map/all_to_all | solution.py:371
  28.6 0.9 %shard_map.68 = bf16[32,1,3,16,128]{4,3,2,1,0:T(8,128)(2,1)} custom-call(bf16[32,1,3,16,128]{4,3,2,1,0:T(8,128)(2,1)S(1)} %bitcast.2), custom_call_target="tpu_custom_call" | custom-call | flops 1048576 | bytes 1572864 | tf_op jit(solution)/shard_map/pallas_call | solution.py:372
  29.6 4.8 %all-to-all-start.1 = ((bf16[32,3,16,128]{3,2,1,0:T(8,128)(2,1)}), bf16[32,3,16,128]{3,2,1,0:T(8,128)(2,1)S(1)}, u32[]{:S(2)}, u32[]{:S(2)}) async-start(bf16[32,3,16,128]{3,2,1,0:T(8,128)(2,1)} %bitcast.1), calls=%async_computation.1 | async-start | bytes 786432 | tf_op jit(solution)/shard_map/all_to_all | solution.py:384
  34.4 0.0 collective-permute-done
  34.4 0.0 collective-permute-done.1
  34.4 0.2 pad_maximum_fusion.edge_ref
  34.6 0.0 copy-done.1
  34.6 0.0 copy-done.3
  34.6 0.0 copy-done.2
  34.6 0.0 copy-start
  34.6 1.0 %copy-done = bf16[4,16,4096]{2,1,0:T(8,128)(2,1)S(1)} copy-done((bf16[4,16,4096]{2,1,0:T(8,128)(2,1)S(1)}, bf16[4,16,4096]{2,1,0:T(8,128)(2,1)}, u32[]{:S(2)}) %copy-start) | copy-done | bytes 524312
  35.6 3.9 %shard_map.69.local_ref = f32[4,3,32,16,128]{4,3,2,1,0:T(8,128)S(1)} custom-call(f32[4]{0:T(128)S(1)} %copy-done.2, f32[4]{0:T(128)S(1)} %copy-done.3, f32[4]{0:T(128)S(1)} %copy-done.1, bf16[4,16,4096]{2,1,0:T(8,128)(2,1)S(1)} %copy-done, bf16[4,8,4096]{2,1,0:T(8,128)(2,1)S(1)} %pad_maximum_fusion.edge_ref), custom_call_target="tpu_custom_call" | custom-call | flops 15728640 | bytes 5242880 | tf_op jit(solution)/shard_map/pallas_call | solution.py:387
  39.6 9.3 %all-to-all-done.1.pre_ref = bf16[32,3,16,128]{3,2,1,0:T(8,128)(2,1)S(1)} async-done(((bf16[32,3,16,128]{3,2,1,0:T(8,128)(2,1)}), bf16[32,3,16,128]{3,2,1,0:T(8,128)(2,1)S(1)}, u32[]{:S(2)}, u32[]{:S(2)}) %all-to-all-start.1) | async-done | bytes 393248 | tf_op jit(solution)/shard_map/all_to_all | solution.py:384
  48.8 0.1 fusion.1
  48.9 0.3 collective-permute-start.3
  49.2 0.2 collective-permute-start.2
  49.4 2.2 %shard_map.70 = (f32[4,3,32,16,128]{4,3,2,1,0:T(8,128)S(1)}, f32[4,8,128]{2,1,0:T(8,128)S(1)}) custom-call(f32[4]{0:T(128)S(1)} %copy-done.1, bf16[32,3,16,128]{3,2,1,0:T(8,128)(2,1)S(1)} %all-to-all-done.1.pre_ref, f32[4,3,32,16,128]{4,3,2,1,0:T(8,128)S(1)} %shard_map.69.local_ref), custom_call_target="tpu_custom_call" | custom-call | flops 7864320 | bytes 5242880 | tf_op jit(solution)/shard_map/pallas_call | solution.py:400
  51.6 0.0 collective-permute-done.3.after_ref
  51.6 2.3 %collective-permute-done.2.before_ref = bf16[32,3,2,128]{3,2,1,0:T(2,128)(2,1)S(1)} collective-permute-done((bf16[32,3,2,128]{3,2,1,0:T(2,128)(2,1)S(1)}, bf16[32,3,2,128]{3,2,1,0:T(2,128)(2,1)S(1)}, u32[]{:S(2)}, u32[]{:S(2)}) %collective-permute-start.2) | collective-permute-done | bytes 49184 | tf_op jit(solution)/shard_map/ppermute | solution.py:398
  54.0 1.7 %shard_map.71 = (bf16[4,16,4096]{2,1,0:T(8,128)(2,1)}, bf16[4,16,4096]{2,1,0:T(8,128)(2,1)}, bf16[4,16,4096]{2,1,0:T(8,128)(2,1)}) custom-call(f32[4,8,128]{2,1,0:T(8,128)S(1)} %get-tuple-element.9.slope_ref, bf16[32,3,2,128]{3,2,1,0:T(2,128)(2,1)S(1)} %collective-permute-done.2.before_ref, bf16[32,3,2,128]{3,2,1,0:T(2,128)(2,1)S(1)} %collective-permute-done.3.after_ref, ...), custom_call_target="tpu_custom_call" | custom-call | flops 10485760 | bytes 5242880 | tf_op jit(solution)/shard_map/pallas_call | solution.py:410
  (1 shorter events, 0.0 us)
Async XLA Ops:
  0.6 33.9 %copy-start.1 = (f32[4]{0:T(128)S(1)}, f32[4]{0:T(128)}, u32[]{:S(2)}) copy-start(f32[4]{0:T(128)} %source_ref.3) | copy-start | bytes 52
  0.6 33.9 %copy-start.3 = (f32[4]{0:T(128)S(1)}, f32[4]{0:T(128)}, u32[]{:S(2)}) copy-start(f32[4]{0:T(128)} %dist_ref.1) | copy-start | bytes 52
  0.7 33.9 %copy-start.2 = (f32[4]{0:T(128)S(1)}, f32[4]{0:T(128)}, u32[]{:S(2)}) copy-start(f32[4]{0:T(128)} %weight_ref.1) | copy-start | bytes 52
  2.6 26.1 %all-to-all-start = ((bf16[32,3,16,128]{3,2,1,0:T(8,128)(2,1)}), bf16[32,3,16,128]{3,2,1,0:T(8,128)(2,1)S(1)}, u32[]{:S(2)}, u32[]{:S(2)}) async-start(bf16[32,3,16,128]{3,2,1,0:T(8,128)(2,1)} %shard_map.67), calls=%async_computation | async-start | bytes 786432 | tf_op jit(solution)/shard_map/all_to_all | solution.py:371
  14.9 19.5 %collective-permute-start = (bf16[4,2,4096]{2,1,0:T(2,128)(2,1)S(1)}, bf16[4,2,4096]{2,1,0:T(2,128)(2,1)S(1)}, u32[]{:S(2)}, u32[]{:S(2)}) collective-permute-start(bf16[4,2,4096]{2,1,0:T(2,128)(2,1)S(1)} %get-tuple-element.11), channel_id=1, source_target_pairs={{1,0},{2,1},{3,2},{4,3},{5,4},{6,5},{7,6},{0,7},{9,8},{10,9},{11,1... | collective-permute-start | bytes 196616 | tf_op jit(solution)/shard_map/ppermute | solution.py:351
  16.8 17.6 %collective-permute-start.1 = (bf16[4,2,4096]{2,1,0:T(2,128)(2,1)S(1)}, bf16[4,2,4096]{2,1,0:T(2,128)(2,1)S(1)}, u32[]{:S(2)}, u32[]{:S(2)}) collective-permute-start(bf16[4,2,4096]{2,1,0:T(2,128)(2,1)S(1)} %get-tuple-element.12), channel_id=1, source_target_pairs={{0,1},{1,2},{2,3},{3,4},{4,5},{5,6},{6,7},{7,0},{8,9},{9,10},{10,1... | collective-permute-start | bytes 196616 | tf_op jit(solution)/shard_map/ppermute | solution.py:350
  29.6 19.3 %all-to-all-start.1 = ((bf16[32,3,16,128]{3,2,1,0:T(8,128)(2,1)}), bf16[32,3,16,128]{3,2,1,0:T(8,128)(2,1)S(1)}, u32[]{:S(2)}, u32[]{:S(2)}) async-start(bf16[32,3,16,128]{3,2,1,0:T(8,128)(2,1)} %bitcast.1), calls=%async_computation.1 | async-start | bytes 786432 | tf_op jit(solution)/shard_map/all_to_all | solution.py:384
  34.6 1.0 %copy-start = (bf16[4,16,4096]{2,1,0:T(8,128)(2,1)S(1)}, bf16[4,16,4096]{2,1,0:T(8,128)(2,1)}, u32[]{:S(2)}) copy-start(bf16[4,16,4096]{2,1,0:T(8,128)(2,1)} %pot_ref.1) | copy-start | bytes 1572868
  48.9 2.7 %collective-permute-start.3 = (bf16[32,3,2,128]{3,2,1,0:T(2,128)(2,1)S(1)}, bf16[32,3,2,128]{3,2,1,0:T(2,128)(2,1)S(1)}, u32[]{:S(2)}, u32[]{:S(2)}) collective-permute-start(bf16[32,3,2,128]{3,2,1,0:T(2,128)(2,1)S(1)} %get-tuple-element.13), channel_id=1, source_target_pairs={{1,0},{2,1},{3,2},{4,3},{5,4},{6,5},{7,6},{0,7},{9,8},{10,9},{11,1... | collective-permute-start | bytes 147464 | tf_op jit(solution)/shard_map/ppermute | solution.py:399
  49.2 4.7 %collective-permute-start.2 = (bf16[32,3,2,128]{3,2,1,0:T(2,128)(2,1)S(1)}, bf16[32,3,2,128]{3,2,1,0:T(2,128)(2,1)S(1)}, u32[]{:S(2)}, u32[]{:S(2)}) collective-permute-start(bf16[32,3,2,128]{3,2,1,0:T(2,128)(2,1)S(1)} %get-tuple-element.14), channel_id=1, source_target_pairs={{0,1},{1,2},{2,3},{3,4},{4,5},{5,6},{6,7},{7,0},{8,9},{9,10},{10,1... | collective-permute-start | bytes 147464 | tf_op jit(solution)/shard_map/ppermute | solution.py:398

commit v6 on v5

--- a/solution.py
+++ b/solution.py
@@ -10,6 +10,7 @@
 LANES = 128
 SUB = 8
 STEPS = 8
+PIECES = 16
 SCALE = 1.0 / 24.0
 SCALE_CROSS = 1.0 / 144.0
 VMEM = pl.BlockSpec(memory_space=pltpu.VMEM)
@@ -283,7 +284,7 @@
 
 def join_kernel(slope_ref, before_ref, after_ref, own_ref, conv_hbm, one_hbm, two_hbm, conv_ref, one_ref, two_ref, field, sems):
     planes, chunks, height = own_ref.shape[0], own_ref.shape[2], own_ref.shape[3]
-    per = chunks // STEPS
+    per = chunks // PIECES
     slope = [slope_ref[s] for s in range(planes)]
     row, lane = iotas()
     tiles = height // SUB
@@ -328,8 +329,8 @@
         return carry
 
     copies = []
-    for i in range(STEPS):
-        lax.fori_loop(i * per, (i + 1) * per, sten, 0, unroll=4)
+    for i in range(PIECES):
+        lax.fori_loop(i * per, (i + 1) * per, sten, 0, unroll=2)
         piece = pl.ds(i * per * LANES, per * LANES)
         for n, (ref, hbm) in enumerate(((conv_ref, conv_hbm), (one_ref, one_hbm), (two_ref, two_hbm))):
             copies.append(pltpu.make_async_copy(ref.at[:, :, piece], hbm.at[:, :, piece], sems.at[n, i]))
@@ -415,7 +416,7 @@
             scratch_shapes=[
                 *[pltpu.VMEM(potentials.shape, BF16)] * 3,
                 pltpu.VMEM((2, chunks, SUB, LANES), F32),
-                pltpu.SemaphoreType.DMA((3, STEPS)),
+                pltpu.SemaphoreType.DMA((3, PIECES)),
             ],
             compiler_params=params(),
             cost_estimate=cost(40 * size, 20 * size),

time: 56.1 us -> 56.3 us (level)
  transfers between devices with their start and end apart: 6 -> 6, of which waited for: 3 -> 3; matrix products, arithmetic and copies ran while one was open for 2% -> 2% of each run, Pallas kernels for 13% -> 12%
where the time goes in v6:
time: 56.3 us; the launch traced here: 55.9 us
  waiting for transfers between devices  23.4 us (42%)
  starting transfers between devices  18.4 us (33%)
  Pallas kernels  10.8 us (19%)
  local copies, waits for them, and re-layouts  2.35 us (4%)
  between operations  0.77 us (1%)
    all_to_all x1, waiting for transfers between devices, on_device(): lax.all_to_all(totals, 'los', split_axis=0, concat_axis=0, tiled=True)  11.7 us
    all_to_all x1, starting transfers between devices, on_device(): lax.all_to_all(totals, 'los', split_axis=0, concat_axis=0, tiled=True)  11.2 us
    all_to_all x1, waiting for transfers between devices, on_device(): lax.all_to_all(earlier.reshape((chunks,) + piece), 'los', split_axis=0, c...  9.29 us
    all_to_all x1, starting transfers between devices, on_device(): lax.all_to_all(earlier.reshape((chunks,) + piece), 'los', split_axis=0, c...  4.79 us
    pallas_call x1, Pallas kernels, on_device(): pl.pallas_call(local_kernel, out_shape=grids, in_specs=[SMEM, SMEM, SMEM,...  3.91 us
    ppermute x1, waiting for transfers between devices, on_device(): pre_before = lax.ppermute(prefix[:, :, height - 2:], 'sky', forward)  2.33 us
    pallas_call x1, Pallas kernels, on_device(): pl.pallas_call(own_kernel, out_shape=[grids, f32(shells, SUB, LANES)], in...  2.16 us
    pallas_call x1, Pallas kernels, on_device(): pl.pallas_call(join_kernel, out_shape=[jax.ShapeDtypeStruct(potentials.sh...  1.95 us
  transfers between devices with their start and end apart: 6, of which 3 were waited for; matrix products, arithmetic and copies ran while one was open for 2% of the time, Pallas kernels for 12%

profile of v6, /device:TPU:32, one launch (start us, length us, event | category | flops | bytes accessed | tf_op | source)
XLA Modules:
  0.0 55.9 jit_solution(13386672055698010732)
XLA Ops:
  0.6 0.0 copy-start.1
  0.6 0.0 copy-start.3
  0.7 0.0 copy-start.2
  0.7 1.9 %shard_map.67 = bf16[32,3,16,128]{3,2,1,0:T(8,128)(2,1)} custom-call(f32[4]{0:T(128)} %weight_ref.1, f32[4]{0:T(128)} %dist_ref.1, f32[4]{0:T(128)} %source_ref.3, bf16[4,16,4096]{2,1,0:T(8,128)(2,1)} %pot_ref.1), custom_call_target="tpu_custom_call" | custom-call | flops 1048576 | bytes 1572864 | tf_op jit(solution)/shard_map/pallas_call | solution.py:356
  2.6 11.2 %all-to-all-start = ((bf16[32,3,16,128]{3,2,1,0:T(8,128)(2,1)}), bf16[32,3,16,128]{3,2,1,0:T(8,128)(2,1)S(1)}, u32[]{:S(2)}, u32[]{:S(2)}) async-start(bf16[32,3,16,128]{3,2,1,0:T(8,128)(2,1)} %shard_map.67), calls=%async_computation | async-start | bytes 786432 | tf_op jit(solution)/shard_map/all_to_all | solution.py:372
  13.8 1.1 %fusion = (bf16[4,2,4096]{2,1,0:T(2,128)(2,1)S(1)}, bf16[4,2,4096]{2,1,0:T(2,128)(2,1)S(1)}) fusion(bf16[4,16,4096]{2,1,0:T(8,128)(2,1)} %pot_ref.1), kind=kLoop, calls=%fused_computation.1 | loop fusion | bytes 262144 | tf_op jit(solution)/shard_map/slice | solution.py:352
  14.9 1.9 %collective-permute-start = (bf16[4,2,4096]{2,1,0:T(2,128)(2,1)S(1)}, bf16[4,2,4096]{2,1,0:T(2,128)(2,1)S(1)}, u32[]{:S(2)}, u32[]{:S(2)}) collective-permute-start(bf16[4,2,4096]{2,1,0:T(2,128)(2,1)S(1)} %get-tuple-element.11), channel_id=1, source_target_pairs={{1,0},{2,1},{3,2},{4,3},{5,4},{6,5},{7,6},{0,7},{9,8},{10,9},{11,1... | collective-permute-start | bytes 196616 | tf_op jit(solution)/shard_map/ppermute | solution.py:352
  16.8 0.0 collective-permute-start.1
  16.8 0.1 pad.1.clone
  16.9 11.7 %all-to-all-done = bf16[32,3,16,128]{3,2,1,0:T(8,128)(2,1)S(1)} async-done(((bf16[32,3,16,128]{3,2,1,0:T(8,128)(2,1)}), bf16[32,3,16,128]{3,2,1,0:T(8,128)(2,1)S(1)}, u32[]{:S(2)}, u32[]{:S(2)}) %all-to-all-start) | async-done | bytes 393248 | tf_op jit(solution)/shard_map/all_to_all | solution.py:372
  28.6 0.9 %shard_map.68 = bf16[32,1,3,16,128]{4,3,2,1,0:T(8,128)(2,1)} custom-call(bf16[32,1,3,16,128]{4,3,2,1,0:T(8,128)(2,1)S(1)} %bitcast.2), custom_call_target="tpu_custom_call" | custom-call | flops 1048576 | bytes 1572864 | tf_op jit(solution)/shard_map/pallas_call | solution.py:373
  29.6 4.8 %all-to-all-start.1 = ((bf16[32,3,16,128]{3,2,1,0:T(8,128)(2,1)}), bf16[32,3,16,128]{3,2,1,0:T(8,128)(2,1)S(1)}, u32[]{:S(2)}, u32[]{:S(2)}) async-start(bf16[32,3,16,128]{3,2,1,0:T(8,128)(2,1)} %bitcast.1), calls=%async_computation.1 | async-start | bytes 786432 | tf_op jit(solution)/shard_map/all_to_all | solution.py:385
  34.4 0.0 collective-permute-done
  34.4 0.0 collective-permute-done.1
  34.4 0.2 pad_maximum_fusion.edge_ref
  34.6 0.0 copy-done.1
  34.6 0.0 copy-done.3
  34.6 0.0 copy-done.2
  34.6 0.0 copy-start
  34.6 1.0 %copy-done = bf16[4,16,4096]{2,1,0:T(8,128)(2,1)S(1)} copy-done((bf16[4,16,4096]{2,1,0:T(8,128)(2,1)S(1)}, bf16[4,16,4096]{2,1,0:T(8,128)(2,1)}, u32[]{:S(2)}) %copy-start) | copy-done | bytes 524312
  35.6 3.9 %shard_map.69.local_ref = f32[4,3,32,16,128]{4,3,2,1,0:T(8,128)S(1)} custom-call(f32[4]{0:T(128)S(1)} %copy-done.2, f32[4]{0:T(128)S(1)} %copy-done.3, f32[4]{0:T(128)S(1)} %copy-done.1, bf16[4,16,4096]{2,1,0:T(8,128)(2,1)S(1)} %copy-done, bf16[4,8,4096]{2,1,0:T(8,128)(2,1)S(1)} %pad_maximum_fusion.edge_ref), custom_call_target="tpu_custom_call" | custom-call | flops 15728640 | bytes 5242880 | tf_op jit(solution)/shard_map/pallas_call | solution.py:388
  39.6 9.3 %all-to-all-done.1.pre_ref = bf16[32,3,16,128]{3,2,1,0:T(8,128)(2,1)S(1)} async-done(((bf16[32,3,16,128]{3,2,1,0:T(8,128)(2,1)}), bf16[32,3,16,128]{3,2,1,0:T(8,128)(2,1)S(1)}, u32[]{:S(2)}, u32[]{:S(2)}) %all-to-all-start.1) | async-done | bytes 393248 | tf_op jit(solution)/shard_map/all_to_all | solution.py:385
  48.8 0.1 fusion.1
  48.9 0.3 collective-permute-start.3
  49.2 0.2 collective-permute-start.2
  49.4 2.2 %shard_map.70 = (f32[4,3,32,16,128]{4,3,2,1,0:T(8,128)S(1)}, f32[4,8,128]{2,1,0:T(8,128)S(1)}) custom-call(f32[4]{0:T(128)S(1)} %copy-done.1, bf16[32,3,16,128]{3,2,1,0:T(8,128)(2,1)S(1)} %all-to-all-done.1.pre_ref, f32[4,3,32,16,128]{4,3,2,1,0:T(8,128)S(1)} %shard_map.69.local_ref), custom_call_target="tpu_custom_call" | custom-call | flops 7864320 | bytes 5242880 | tf_op jit(solution)/shard_map/pallas_call | solution.py:401
  51.6 0.0 collective-permute-done.3.after_ref
  51.6 2.3 %collective-permute-done.2.before_ref = bf16[32,3,2,128]{3,2,1,0:T(2,128)(2,1)S(1)} collective-permute-done((bf16[32,3,2,128]{3,2,1,0:T(2,128)(2,1)S(1)}, bf16[32,3,2,128]{3,2,1,0:T(2,128)(2,1)S(1)}, u32[]{:S(2)}, u32[]{:S(2)}) %collective-permute-start.2) | collective-permute-done | bytes 49184 | tf_op jit(solution)/shard_map/ppermute | solution.py:399
  54.0 2.0 %shard_map.71 = (bf16[4,16,4096]{2,1,0:T(8,128)(2,1)}, bf16[4,16,4096]{2,1,0:T(8,128)(2,1)}, bf16[4,16,4096]{2,1,0:T(8,128)(2,1)}) custom-call(f32[4,8,128]{2,1,0:T(8,128)S(1)} %get-tuple-element.9.slope_ref, bf16[32,3,2,128]{3,2,1,0:T(2,128)(2,1)S(1)} %collective-permute-done.2.before_ref, bf16[32,3,2,128]{3,2,1,0:T(2,128)(2,1)S(1)} %collective-permute-done.3.after_ref, ...), custom_call_target="tpu_custom_call" | custom-call | flops 10485760 | bytes 5242880 | tf_op jit(solution)/shard_map/pallas_call | solution.py:411
  (1 shorter events, 0.0 us)
Async XLA Ops:
  0.6 33.9 %copy-start.1 = (f32[4]{0:T(128)S(1)}, f32[4]{0:T(128)}, u32[]{:S(2)}) copy-start(f32[4]{0:T(128)} %source_ref.3) | copy-start | bytes 52
  0.6 33.9 %copy-start.3 = (f32[4]{0:T(128)S(1)}, f32[4]{0:T(128)}, u32[]{:S(2)}) copy-start(f32[4]{0:T(128)} %dist_ref.1) | copy-start | bytes 52
  0.7 33.9 %copy-start.2 = (f32[4]{0:T(128)S(1)}, f32[4]{0:T(128)}, u32[]{:S(2)}) copy-start(f32[4]{0:T(128)} %weight_ref.1) | copy-start | bytes 52
  2.6 26.1 %all-to-all-start = ((bf16[32,3,16,128]{3,2,1,0:T(8,128)(2,1)}), bf16[32,3,16,128]{3,2,1,0:T(8,128)(2,1)S(1)}, u32[]{:S(2)}, u32[]{:S(2)}) async-start(bf16[32,3,16,128]{3,2,1,0:T(8,128)(2,1)} %shard_map.67), calls=%async_computation | async-start | bytes 786432 | tf_op jit(solution)/shard_map/all_to_all | solution.py:372
  14.9 19.5 %collective-permute-start = (bf16[4,2,4096]{2,1,0:T(2,128)(2,1)S(1)}, bf16[4,2,4096]{2,1,0:T(2,128)(2,1)S(1)}, u32[]{:S(2)}, u32[]{:S(2)}) collective-permute-start(bf16[4,2,4096]{2,1,0:T(2,128)(2,1)S(1)} %get-tuple-element.11), channel_id=1, source_target_pairs={{1,0},{2,1},{3,2},{4,3},{5,4},{6,5},{7,6},{0,7},{9,8},{10,9},{11,1... | collective-permute-start | bytes 196616 | tf_op jit(solution)/shard_map/ppermute | solution.py:352
  16.8 17.6 %collective-permute-start.1 = (bf16[4,2,4096]{2,1,0:T(2,128)(2,1)S(1)}, bf16[4,2,4096]{2,1,0:T(2,128)(2,1)S(1)}, u32[]{:S(2)}, u32[]{:S(2)}) collective-permute-start(bf16[4,2,4096]{2,1,0:T(2,128)(2,1)S(1)} %get-tuple-element.12), channel_id=1, source_target_pairs={{0,1},{1,2},{2,3},{3,4},{4,5},{5,6},{6,7},{7,0},{8,9},{9,10},{10,1... | collective-permute-start | bytes 196616 | tf_op jit(solution)/shard_map/ppermute | solution.py:351
  29.6 19.3 %all-to-all-start.1 = ((bf16[32,3,16,128]{3,2,1,0:T(8,128)(2,1)}), bf16[32,3,16,128]{3,2,1,0:T(8,128)(2,1)S(1)}, u32[]{:S(2)}, u32[]{:S(2)}) async-start(bf16[32,3,16,128]{3,2,1,0:T(8,128)(2,1)} %bitcast.1), calls=%async_computation.1 | async-start | bytes 786432 | tf_op jit(solution)/shard_map/all_to_all | solution.py:385
  34.6 1.0 %copy-start = (bf16[4,16,4096]{2,1,0:T(8,128)(2,1)S(1)}, bf16[4,16,4096]{2,1,0:T(8,128)(2,1)}, u32[]{:S(2)}) copy-start(bf16[4,16,4096]{2,1,0:T(8,128)(2,1)} %pot_ref.1) | copy-start | bytes 1572868
  48.9 2.7 %collective-permute-start.3 = (bf16[32,3,2,128]{3,2,1,0:T(2,128)(2,1)S(1)}, bf16[32,3,2,128]{3,2,1,0:T(2,128)(2,1)S(1)}, u32[]{:S(2)}, u32[]{:S(2)}) collective-permute-start(bf16[32,3,2,128]{3,2,1,0:T(2,128)(2,1)S(1)} %get-tuple-element.13), channel_id=1, source_target_pairs={{1,0},{2,1},{3,2},{4,3},{5,4},{6,5},{7,6},{0,7},{9,8},{10,9},{11,1... | collective-permute-start | bytes 147464 | tf_op jit(solution)/shard_map/ppermute | solution.py:400
  49.2 4.7 %collective-permute-start.2 = (bf16[32,3,2,128]{3,2,1,0:T(2,128)(2,1)S(1)}, bf16[32,3,2,128]{3,2,1,0:T(2,128)(2,1)S(1)}, u32[]{:S(2)}, u32[]{:S(2)}) collective-permute-start(bf16[32,3,2,128]{3,2,1,0:T(2,128)(2,1)S(1)} %get-tuple-element.14), channel_id=1, source_target_pairs={{0,1},{1,2},{2,3},{3,4},{4,5},{5,6},{6,7},{7,0},{8,9},{9,10},{10,1... | collective-permute-start | bytes 147464 | tf_op jit(solution)/shard_map/ppermute | solution.py:399
